TPU v7x, 256 devices: a whole 4x4x8 slice. The times are simulated.
256 devices in a mesh: strike: 16 (over z, y_hi), dip: 4 (over x), depth: 4 (over y_lo, core).
Axes of the slice: x: 4, y: 4 (y_hi: 2, y_lo: 2; y = y_hi * 2 + y_lo), z: 8, core: 2. Of those that a mesh axis runs over, the one named last changes fastest.
Arguments:
- velocity: float32 [3, 256, 128, 512], P(None, 'strike', 'dip', 'depth'), may hold values from -6 to 6
- stress: float32 [6, 256, 128, 512], P(None, 'strike', 'dip', 'depth'), may hold values from -6 to 6
- memory: float32 [6, 256, 128, 512], P(None, 'strike', 'dip', 'depth'), may hold values from -4 to 4
- lame_lambda: float32 [256, 128, 512], P('strike', 'dip', 'depth'), may hold values from 0.5 to 2
- shear_modulus: float32 [256, 128, 512], P('strike', 'dip', 'depth'), may hold values from 0.5 to 2
- buoyancy: float32 [256, 128, 512], P('strike', 'dip', 'depth'), may hold values from 0.5 to 2
- relax: float32 [256, 128, 512], P('strike', 'dip', 'depth'), may hold values from 0.2 to 0.95
- anelastic: float32 [256, 128, 512], P('strike', 'dip', 'depth'), may hold values from 0.1 to 1
- moment_rate: float32 [16, 32, 6, 2048], P('strike'), may hold values from -6 to 6
- subfault_cell: int32 [16, 2048], replicated, may hold values from 0 to 131071, as said below
- active_segment: int32 [2], replicated, may hold values from 0 to 15
- stf_offset: int32 [2], replicated, may hold values from 0 to 24
Outputs:
- velocity_out: float32 [3, 256, 128, 512], P(None, 'strike', 'dip', 'depth')
- stress_out: float32 [6, 256, 128, 512], P(None, 'strike', 'dip', 'depth')
- memory_out: float32 [6, 256, 128, 512], P(None, 'strike', 'dip', 'depth')
Inputs may be any that keep to these rules, and one draw needn't show every extreme that they name: subfault_cell[s, j] = x * 512 + z names strike cell x and depth cell z of subfault j of segment s; the subfaults of every segment lie along the whole strike extent, every block of 16 strike cells holding some of them; several subfaults may share a cell.
All inputs are finite; a program needn't handle non-finite values.
Results may differ from a plain program's by a relative error of at most 0.0003.
Values sent between devices are 32-bit elements; how exact they have to be, the bound alone decides.
A program may use at most 64 MiB of HBM per device.

v0:
```python
import functools

import jax
import jax.numpy as jnp
from jax import lax
from jax.experimental import pallas as pl
from jax.experimental.pallas import tpu as pltpu
from jax.sharding import PartitionSpec as P

MESH = pl.DeviceIdType.MESH
TB = 8
STEPS = 2
R24 = 0.12 / 24.0
XP = 2
YP = 8
NA = 2

X_GROUPS = {"s": ((0, 1, 1, 2), (3, 2, 2, 1)), "v": ((0, 1, 2, 1), (1, 2, 1, 2))}
Y_FIELDS = {"s": ((3, True), (5, True), (1, False)), "v": ((1, True), (0, False), (2, False))}
Z_FIELDS = {"s": (4, 5, 2), "v": (0, 1, 2)}
Z_BACK = {"s": (True, True, False), "v": (False, False, True)}


def stress_tiles(x, m, sizes, Sf, Vf, M, deep, material, put):
    CY, ROW = sizes
    for j in range(0, CY, 8):
        at = (x + XP) * ROW + YP + j
        rows = pl.ds(j, 8)

        def get(c, n, at=at):
            return Vf[c, pl.ds(at + n, 8), :]

        vx = [get(0, n * ROW) for n in range(-2, 3)]
        vy = [get(1, n * ROW) for n in range(-1, 4)]
        vz = [get(2, n * ROW) for n in range(-1, 4)]
        for p in range(2):
            o = p * ROW
            lam, mu, relax, ane = material(m + p, rows)
            shear = R24 * mu
            twice = 2.0 * shear
            part = (1.0 - relax) * ane
            vx_at, vy_at, vz_at = vx[2 + p], vy[1 + p], vz[1 + p]
            xx = 27.0 * (vx_at - vx[1 + p]) - (vx[3 + p] - vx[p])
            yy = 27.0 * (vy_at - get(1, o - 1)) - (get(1, o + 1) - get(1, o - 2))
            zz = deep[2, x + p, rows, :]
            normal = R24 * lam * (xx + yy + zz)
            xy = 27.0 * ((get(0, o + 1) - vx_at) + (vy[2 + p] - vy_at)) - (
                (get(0, o + 2) - get(0, o - 1)) + (vy[3 + p] - vy[p]))
            xz = 27.0 * (vz[2 + p] - vz_at) - (vz[3 + p] - vz[p]) + deep[0, x + p, rows, :]
            yz = 27.0 * (get(2, o + 1) - vz_at) - (get(2, o + 2) - get(2, o - 1)) + deep[1, x + p, rows, :]
            grown = (
                normal + twice * xx, normal + twice * yy, normal + twice * zz,
                shear * xy, shear * xz, shear * yz,
            )
            for c in range(6):
                old = M[c, x + p, rows, :]
                new = relax * old + part * grown[c]
                stress = Sf[c, pl.ds(pl.multiple_of(at + o, 8), 8), :] + grown[c] - 0.5 * (old + new)
                put(c, x + p, at + o, rows, stress, new)


def finish(dims, S, V, M, deep, edge, plane, vel_out, str_out, mem_out, stress, memory, sem):
    CX, CY = dims
    ROW = CY + 2 * YP
    own = pl.ds(YP, CY)
    middle = pl.ds(2, CX - 4)
    copies = [
        pltpu.make_async_copy(V.at[:, pl.ds(XP, CX), own], vel_out, sem.at[0]),
        pltpu.make_async_copy(S.at[:, pl.ds(XP + 2, CX - 4), own], str_out.at[:, middle], sem.at[1]),
        pltpu.make_async_copy(M.at[:, middle], mem_out.at[:, middle], sem.at[2]),
    ]
    for copy in copies:
        copy.start()
    Sf = S.reshape(6, (CX + 2 * XP) * ROW, 128)
    Vf = V.reshape(3, (CX + 2 * XP) * ROW, 128)

    @pl.loop(0, 2)
    def _(i):
        x = i * (CX - 2)

        def material(m, rows):
            return tuple(edge[n, m, rows, :] for n in range(4))

        def put(c, at_x, at, rows, s, m):
            place = at_x - i * (CX - 4)
            stress[c, place, rows, :] = s
            memory[c, place, rows, :] = m

        stress_tiles(x, 2 * i, (CY, ROW), Sf, Vf, M, deep, material, put)

    for c in range(6):
        for n, x in enumerate((0, 1, CX - 2, CX - 1)):
            stress[c, n, 0:1, :] = stress[c, n, 0:1, :] - plane[c * CX + x:c * CX + x + 1, :]
    for n in range(2):
        here, there = pl.ds(2 * n, 2), pl.ds(n * (CX - 2), 2)
        copies.append(pltpu.make_async_copy(stress.at[:, here], str_out.at[:, there], sem.at[3 + 2 * n]))
        copies.append(pltpu.make_async_copy(memory.at[:, here], mem_out.at[:, there], sem.at[4 + 2 * n]))
    for copy in copies[3:]:
        copy.start()
    for copy in copies:
        copy.wait()


def kernel(
    dims,
    vel_hbm, str_hbm, mem_hbm, lam_hbm, mu_hbm, buo_hbm, rel_hbm, ane_hbm, rate_hbm, cell_hbm,
    active_hbm, offset_hbm,
    S, V, M, deep, edge, last_plane,
    lam, mu, buo, rel, ane, rate, cells, active, offset,
    ysend_up, ysend_dn, yrecv_up, yrecv_dn, zsend, zrecv_up, zrecv_dn, band,
    cand, pair, chosen, gathered, acc, plane,
    ld_sem, xs_sem, xr_sem, ys_sem, yr_sem, zs_sem, zr_sem,
    c_send, c_recv, p_send, p_recv, g_send, g_recv,
):
    NS, ND, NH, CX, CY, SUBF = dims
    ROW = CY + 2 * YP
    NB = NS // NA
    s = lax.axis_index("strike")
    k = lax.axis_index("dip")
    d = lax.axis_index("depth")
    fault = ND // 2
    on_fault = k == fault
    group, parity = lax.div(s, NA), lax.rem(s, NA)
    chunk = k * NH + d

    def near(axis, pos, size, step):
        return {axis: jnp.clip(pos + step, 0, size - 1)}

    s_up, s_dn = near("strike", s, NS, 1), near("strike", s, NS, -1)
    k_up, k_dn = near("dip", k, ND, 1), near("dip", k, ND, -1)
    d_up, d_dn = near("depth", d, NH, 1), near("depth", d, NH, -1)
    has = {
        "s_up": s < NS - 1, "s_dn": s > 0,
        "k_up": k < ND - 1, "k_dn": k > 0,
        "d_up": d < NH - 1, "d_dn": d > 0,
    }

    inner = (slice(None), pl.ds(XP, CX), pl.ds(YP, CY))
    loads = [
        pltpu.make_async_copy(str_hbm, S.at[inner], ld_sem.at[0]),
        pltpu.make_async_copy(
            rate_hbm.at[0, :, :, pl.ds(pl.multiple_of(chunk * 128, 128), 128)], rate, ld_sem.at[1]
        ),
        pltpu.make_async_copy(vel_hbm, V.at[inner], ld_sem.at[2]),
        pltpu.make_async_copy(buo_hbm, buo, ld_sem.at[3]),
        pltpu.make_async_copy(mem_hbm, M, ld_sem.at[4]),
        pltpu.make_async_copy(lam_hbm, lam, ld_sem.at[5]),
        pltpu.make_async_copy(mu_hbm, mu, ld_sem.at[6]),
        pltpu.make_async_copy(rel_hbm, rel, ld_sem.at[7]),
        pltpu.make_async_copy(ane_hbm, ane, ld_sem.at[8]),
        pltpu.make_async_copy(cell_hbm, cells, ld_sem.at[9]),
    ]
    for n, ref in enumerate((lam_hbm, mu_hbm, rel_hbm, ane_hbm)):
        for m in range(2):
            loads.append(pltpu.make_async_copy(
                ref.at[pl.ds(m * (CX - 2), 2)], edge.at[n, pl.ds(2 * m, 2)], ld_sem.at[10 + 2 * n + m]))
    order = (
        pltpu.make_async_copy(active_hbm, active, ld_sem.at[18]),
        pltpu.make_async_copy(offset_hbm, offset, ld_sem.at[19]),
    )
    for copy in (loads[0], *order, *loads[1:]):
        copy.start()

    barrier = pltpu.get_barrier_semaphore()
    count = jnp.int32(0)
    for name, to in (("s_up", s_up), ("s_dn", s_dn), ("k_up", k_up), ("k_dn", k_dn), ("d_up", d_up), ("d_dn", d_dn)):
        there = has[name]
        count = count + there.astype(jnp.int32)

        @pl.when(there)
        def _(to=to):
            pl.semaphore_signal(barrier, inc=1, device_id=to, device_id_type=MESH)

    other = {"strike": group * NA + lax.rem(parity + 1, NA)}
    pl.semaphore_signal(barrier, inc=1, device_id=other, device_id_type=MESH)
    count = count + 1

    @pl.loop(0, NB)
    def _(g):
        @pl.when(g != group)
        def _():
            pl.semaphore_signal(
                barrier, inc=1, device_id={"strike": g * NA + parity}, device_id_type=MESH
            )

    count = count + (NB - 1)

    @pl.loop(0, NH)
    def _(h):
        @pl.when(jnp.logical_not(on_fault & (h == d)))
        def _():
            pl.semaphore_signal(
                barrier, inc=1, device_id={"dip": fault, "depth": h}, device_id_type=MESH
            )

    count = count + NH - on_fault.astype(jnp.int32)

    @pl.when(on_fault)
    def _():
        @pl.loop(0, ND * NH)
        def _(j):
            @pl.when(j != chunk)
            def _():
                pl.semaphore_signal(
                    barrier, inc=1,
                    device_id={"dip": lax.div(j, NH), "depth": lax.rem(j, NH)},
                    device_id_type=MESH,
                )

    count = count + jnp.where(on_fault, ND * NH - 1, 0)
    pl.semaphore_wait(barrier, count)

    def x_copies(h):
        kind = "sv"[h % 2]
        ref = S if kind == "s" else V
        up, dn = [], []
        for n, (c0, nc, lu, ld) in enumerate(X_GROUPS[kind]):
            comps = pl.ds(c0, nc)
            rows = pl.ds(YP, CY)
            if h == 0:
                src_up = str_hbm.at[comps, pl.ds(CX - lu, lu)]
                src_dn = str_hbm.at[comps, pl.ds(0, ld)]
            else:
                src_up = ref.at[comps, pl.ds(XP + CX - lu, lu), rows]
                src_dn = ref.at[comps, pl.ds(XP, ld), rows]
            up.append(pltpu.make_async_remote_copy(
                src_up, ref.at[comps, pl.ds(XP - lu, lu), rows],
                xs_sem.at[h, n], xr_sem.at[h, n], device_id=s_up, device_id_type=MESH))
            dn.append(pltpu.make_async_remote_copy(
                src_dn, ref.at[comps, pl.ds(XP + CX, ld), rows],
                xs_sem.at[h, 2 + n], xr_sem.at[h, 2 + n], device_id=s_dn, device_id_type=MESH))
        return up, dn

    def each(there, copies, act):
        @pl.when(there)
        def _():
            for copy in copies:
                act(copy)

    def x_start(h):
        up, dn = x_copies(h)
        each(has["s_up"], up, lambda c: c.start())
        each(has["s_dn"], dn, lambda c: c.start())

    def x_wait_recv(h):
        up, dn = x_copies(h)
        each(has["s_dn"], up, lambda c: c.wait_recv())
        each(has["s_up"], dn, lambda c: c.wait_recv())

    def x_wait_send(h):
        up, dn = x_copies(h)
        each(has["s_up"], up, lambda c: c.wait_send())
        each(has["s_dn"], dn, lambda c: c.wait_send())

    x_start(0)

    Sf = S.reshape(6, (CX + 2 * XP) * ROW, 128)
    Vf = V.reshape(3, (CX + 2 * XP) * ROW, 128)
    flat = {"s": Sf, "v": Vf}

    for F, nc in ((S, 6), (V, 3)):
        zero_x = jnp.zeros((nc, XP, CY, 128), jnp.float32)

        @pl.when(s == 0)
        def _(F=F, zero_x=zero_x):
            F[:, 0:XP, YP:YP + CY, :] = zero_x

        @pl.when(s == NS - 1)
        def _(F=F, zero_x=zero_x):
            F[:, XP + CX:, YP:YP + CY, :] = zero_x

    zero_y = jnp.zeros(yrecv_up.shape, jnp.float32)
    zero_z = jnp.zeros(zrecv_up.shape, jnp.float32)
    for there, ref, zero in (
        (has["k_dn"], yrecv_up, zero_y), (has["k_up"], yrecv_dn, zero_y),
        (has["d_dn"], zrecv_up, zero_z), (has["d_up"], zrecv_dn, zero_z),
    ):
        @pl.when(jnp.logical_not(there))
        def _(ref=ref, zero=zero):
            ref[...] = zero

    def y_layers(kind):
        up, dn = [], []
        for c, back in Y_FIELDS[kind]:
            up += [(c, CY - 2), (c, CY - 1)] if back else [(c, CY - 1)]
            dn += [(c, 0)] if back else [(c, 0), (c, 1)]
        return up, dn

    def y_copies(h):
        up, dn = y_layers("sv"[h % 2])
        nu, nd = len(up), len(dn)
        return (
            pltpu.make_async_remote_copy(
                ysend_up.at[h, pl.ds(0, nu)], yrecv_up.at[h, pl.ds(0, nu)],
                ys_sem.at[h, 0], yr_sem.at[h, 0], device_id=k_up, device_id_type=MESH),
            pltpu.make_async_remote_copy(
                ysend_dn.at[h, pl.ds(0, nd)], yrecv_dn.at[h, pl.ds(0, nd)],
                ys_sem.at[h, 1], yr_sem.at[h, 1], device_id=k_dn, device_id_type=MESH),
        )

    def z_copies(h):
        return (
            pltpu.make_async_remote_copy(
                zsend.at[h], zrecv_up.at[h],
                zs_sem.at[h, 0], zr_sem.at[h, 0], device_id=d_up, device_id_type=MESH),
            pltpu.make_async_remote_copy(
                zsend.at[h], zrecv_dn.at[h],
                zs_sem.at[h, 1], zr_sem.at[h, 1], device_id=d_dn, device_id_type=MESH),
        )

    lane = lax.broadcasted_iota(jnp.int32, (CY, 128), 1)
    slot = lane >> 2
    quarter = lane & 3

    def turn(value, n):
        return pltpu.roll(value, n % 128, 1)

    def yz_send(h):
        kind = "sv"[h % 2]
        F = flat[kind]
        up, dn = y_layers(kind)
        base = XP * ROW + YP
        for n, (c, row) in enumerate(up):
            ysend_up[h, n] = F[c, pl.ds(base + row, CX, stride=ROW), :]
        for n, (c, row) in enumerate(dn):
            ysend_dn[h, n] = F[c, pl.ds(base + row, CX, stride=ROW), :]
        up, dn = y_copies(h)
        each(has["k_up"], [up], lambda c: c.start())
        each(has["k_dn"], [dn], lambda c: c.start())

        first = second = jnp.zeros((CY, 128), jnp.float32)
        for x in range(CX):
            a, b, c = (F[comp, pl.ds((x + XP) * ROW + YP, CY), :] for comp in Z_FIELDS[kind])
            first = jnp.where(slot == x, turn(a, 4 * x + 2), first)
            first = jnp.where(slot == x + CX, turn(b, 4 * x + 66), first)
            second = jnp.where(slot == x, turn(c, 4 * x + 2), second)
        zsend[h, 0] = first
        zsend[h, 1] = second
        up, dn = z_copies(h)
        each(has["d_up"], [up], lambda c: c.start())
        each(has["d_dn"], [dn], lambda c: c.start())

    def yz_recv(h):
        kind = "sv"[h % 2]
        F = flat[kind]
        up, dn = y_copies(h)
        each(has["k_dn"], [up], lambda c: c.wait_recv())
        each(has["k_up"], [dn], lambda c: c.wait_recv())
        up, dn = y_layers(kind)
        base = XP * ROW + YP
        for n, (c, row) in enumerate(up):
            F[c, pl.ds(base + row - CY, CX, stride=ROW), :] = yrecv_up[h, n]
        for n, (c, row) in enumerate(dn):
            F[c, pl.ds(base + row + CY, CX, stride=ROW), :] = yrecv_dn[h, n]
        up, dn = z_copies(h)
        each(has["d_dn"], [up], lambda c: c.wait_recv())
        each(has["d_up"], [dn], lambda c: c.wait_recv())
        fixes = []
        for n in range(2):
            mix = jnp.where(quarter < 2, zrecv_up[h, n], zrecv_dn[h, n])
            below, two_after = turn(mix, 1), turn(mix, -2)
            if Z_BACK[kind][2 * n]:
                fix = jnp.where(quarter == 0, -two_after, jnp.where(quarter == 1, below - 27.0 * mix, below))
            else:
                fix = jnp.where(quarter == 1, 27.0 * turn(mix, -1) - two_after, jnp.where(quarter == 0, -two_after, below))
            fixes.append(jnp.where(quarter == 3, 0.0, fix))
        for place, back in enumerate(Z_BACK[kind]):
            ends = (lane == 127) | (lane < 2) if back else (lane > 125) | (lane == 0)
            for x in range(CX):
                moved = turn(fixes[place // 2], (127 if back else 126) - 4 * x - 64 * (place % 2))
                deep[place, x] = deep[place, x] + jnp.where(ends, moved, 0.0)

    def deep_all(h):
        kind = "sv"[h % 2]
        F = S if kind == "s" else V
        for place, (comp, back) in enumerate(zip(Z_FIELDS[kind], Z_BACK[kind])):
            f = F[comp, XP:XP + CX, YP:YP + CY, :].reshape(CX * CY, 128)
            high = f.astype(jnp.bfloat16)
            low = (f - high.astype(jnp.float32)).astype(jnp.bfloat16)
            out = lax.dot_general(
                jnp.concatenate([high, low], axis=1), band[1 if back else 0],
                (((1,), (0,)), ((), ())), preferred_element_type=jnp.float32)
            deep[place] = out.reshape(CX, CY, 128)

    def velocity_pair(x):
        for j in range(0, CY, 8):
            at = (x + XP) * ROW + YP + j

            def get(c, n, Sf=Sf, at=at):
                return Sf[c, pl.ds(at + n, 8), :]

            xx = [get(0, n * ROW) for n in range(-1, 4)]
            xy = [get(3, n * ROW) for n in range(-2, 3)]
            xz = [get(4, n * ROW) for n in range(-2, 3)]
            for p in range(2):
                o = p * ROW
                gain = R24 * buo[x + p, pl.ds(j, 8), :]
                xy_at, yy, yz = xy[2 + p], [get(1, o + n) for n in range(-1, 3)], [get(5, o + n) for n in range(-2, 2)]
                close = (
                    (xx[2 + p] - xx[1 + p]) + (xy_at - get(3, o - 1)),
                    (xy_at - xy[1 + p]) + (yy[2] - yy[1]),
                    (xz[2 + p] - xz[1 + p]) + (yz[2] - yz[1]),
                )
                far = (
                    (xx[3 + p] - xx[p]) + (get(3, o + 1) - get(3, o - 2)),
                    (xy[3 + p] - xy[p]) + (yy[3] - yy[0]),
                    (xz[3 + p] - xz[p]) + (yz[3] - yz[0]),
                )
                for c in range(3):
                    own = pl.ds(pl.multiple_of(at + o, 8), 8)
                    Vf[c, own, :] = Vf[c, own, :] + gain * (
                        27.0 * close[c] - far[c] + deep[c, x + p, pl.ds(j, 8), :])

    def stress_pair(x):
        def material(x, rows):
            return lam[x, rows, :], mu[x, rows, :], rel[x, rows, :], ane[x, rows, :]

        def put(c, x, at, rows, stress, memory):
            Sf[c, pl.ds(pl.multiple_of(at, 8), 8), :] = stress
            M[c, x, rows, :] = memory

        stress_tiles(x, x, (CY, ROW), Sf, Vf, M, deep, material, put)

    def interior(one):
        @pl.loop(0, (CX - 4) // 2)
        def _(i):
            one(2 * i + 2)

    def boundary(one):
        @pl.loop(0, 2)
        def _(i):
            one(i * (CX - 2))

    def candidates():
        row = lax.broadcasted_iota(jnp.int32, (TB, 128), 0)
        weights = jnp.where((row == 0) | (row == TB - 1), 0.5 / (TB - 1), 1.0 / (TB - 1))
        for t in range(STEPS):
            o = offset[t]
            for c in range(6):
                samples = rate[c, pl.ds(o, TB), :]
                cand[group, t, c:c + 1, :] = jnp.sum(samples * weights, axis=0, keepdims=True)
            cand[group, t, 6:8, :] = jnp.zeros((2, 128), jnp.float32)

    def c_copy(sender, receiver):
        return pltpu.make_async_remote_copy(
            cand.at[sender], cand.at[sender], c_send.at[receiver], c_recv.at[sender],
            device_id={"strike": receiver * NA + parity}, device_id_type=MESH)

    def over_groups(act):
        @pl.loop(0, NB)
        def _(g):
            @pl.when(g != group)
            def _():
                act(g)

    def pair_copy(which):
        return pltpu.make_async_remote_copy(
            pair.at[which], pair.at[which], p_send, p_recv, device_id=other, device_id_type=MESH)

    def g_copy(which, h):
        return pltpu.make_async_remote_copy(
            chosen, gathered.at[which], g_send.at[h], g_recv.at[which],
            device_id={"dip": fault, "depth": h}, device_id_type=MESH)

    def over_fault(act):
        @pl.loop(0, NH)
        def _(h):
            @pl.when(jnp.logical_not(on_fault & (h == d)))
            def _():
                act(h)

    def source_first():
        loads[1].wait()
        for copy in order:
            copy.wait()
        candidates()
        over_groups(lambda g: c_copy(group, g).start())

    def source_second():
        over_groups(lambda g: c_copy(g, group).wait_recv())
        for t in range(STEPS):
            pair[parity, t] = cand[lax.div(active[t], NA), t]
        pair_copy(parity).start()

    def source_third():
        pair_copy(lax.rem(parity + 1, NA)).wait_recv()
        for t in range(STEPS):
            value = pair[lax.rem(active[t], NA), t]
            chosen[t] = value

            @pl.when(on_fault)
            def _(t=t, value=value):
                gathered[chunk, t] = value

        over_fault(lambda h: g_copy(chunk, h).start())

    def source_gather():
        @pl.when(on_fault)
        def _():
            @pl.loop(0, ND * NH)
            def _(j):
                @pl.when(j != chunk)
                def _():
                    g_copy(j, 0).wait_recv()

    def source_plane(t):
        @pl.when(on_fault)
        def _():
            seg = active[t]
            depth_total = 128 * NH
            acc[...] = jnp.zeros_like(acc)
            wide = 8 * 128

            @pl.loop(0, SUBF // wide)
            def _(i):
                cell = cells[pl.ds(seg, 1), pl.ds(pl.multiple_of(i * wide, wide), wide)]
                cell_x = lax.div(cell, depth_total)
                cell_z = cell - cell_x * depth_total - d * 128
                cell_x = cell_x - s * CX
                hot_z = (lax.broadcasted_iota(jnp.int32, (128, wide), 0) == cell_z).astype(jnp.float32).astype(jnp.bfloat16)
                hot_x = lax.broadcasted_iota(jnp.int32, (CX, wide), 0) == cell_x
                value = jnp.concatenate([gathered[8 * i + n, t] for n in range(8)], axis=1)
                parts = []
                for _ in range(3):
                    part = value.astype(jnp.bfloat16).astype(jnp.float32)
                    parts.append(part)
                    value = value - part
                rows = [
                    jnp.where(hot_x, part[c:c + 1, :], 0.0).astype(jnp.bfloat16)
                    for part in parts for c in range(6)
                ]
                acc[...] += lax.dot_general(
                    jnp.concatenate(rows, axis=0), hot_z, (((1,), (1,)), ((), ())),
                    preferred_element_type=jnp.float32)

            n = 6 * CX
            (plane if t == 0 else last_plane)[...] = acc[0:n] + acc[n:2 * n] + acc[2 * n:3 * n]

    def apply_source(ref, spans):
        @pl.when(on_fault)
        def _():
            for c in range(6):
                for x0, n in spans:
                    at = pl.ds((x0 + XP) * ROW + YP, n, stride=ROW)
                    Sf[c, at, :] = Sf[c, at, :] - ref[c * CX + x0:c * CX + x0 + n, :]

    edges = ((0, 2), (CX - 2, 2))
    middle = ((2, CX - 4),)

    i, j = (lax.broadcasted_iota(jnp.int32, (256, 128), n) for n in range(2))
    off = (i & 127) - j
    for n, (a, b) in enumerate(((1, 0), (0, -1))):
        weight = jnp.where(off == a, 27.0, jnp.where(off == b, -27.0, jnp.where(
            off == a + 1, -1.0, jnp.where(off == b - 1, 1.0, 0.0))))
        band[n] = weight.astype(jnp.bfloat16)

    @pl.when(jnp.logical_not(on_fault))
    def _():
        last_plane[...] = jnp.zeros_like(last_plane)

    loads[0].wait()
    yz_send(0)
    source_first()
    deep_all(0)
    loads[2].wait()
    loads[3].wait()
    yz_recv(0)
    interior(velocity_pair)
    source_second()
    x_wait_recv(0)
    boundary(velocity_pair)
    x_start(1)
    yz_send(1)
    source_third()
    deep_all(1)
    for copy in loads[4:]:
        copy.wait()
    yz_recv(1)
    interior(stress_pair)
    source_gather()
    source_plane(0)
    apply_source(plane, middle)
    x_wait_recv(1)
    x_wait_send(0)
    boundary(stress_pair)
    apply_source(plane, edges)
    x_start(2)
    yz_send(2)
    deep_all(2)
    source_plane(1)
    x_wait_send(1)
    yz_recv(2)
    interior(velocity_pair)
    x_wait_recv(2)
    boundary(velocity_pair)
    x_start(3)
    yz_send(3)
    deep_all(3)
    yz_recv(3)
    interior(stress_pair)
    apply_source(last_plane, middle)
    x_wait_recv(3)

    x_wait_send(2)
    x_wait_send(3)
    for h in range(4):
        up, dn = y_copies(h)
        each(has["k_up"], [up], lambda c: c.wait_send())
        each(has["k_dn"], [dn], lambda c: c.wait_send())
        up, dn = z_copies(h)
        each(has["d_up"], [up], lambda c: c.wait_send())
        each(has["d_dn"], [dn], lambda c: c.wait_send())
    over_groups(lambda g: c_copy(group, g).wait_send())
    pair_copy(parity).wait_send()
    over_fault(lambda h: g_copy(chunk, h).wait_send())


def solution(mesh):
    ns, nd, nh = (mesh.shape[a] for a in ("strike", "dip", "depth"))

    def body(velocity, stress, memory, lam, mu, buo, rel, ane, rate, cell, active, offset):
        cx, cy, cz = lam.shape
        subf = cell.shape[1]
        assert cz == 128 and subf == 128 * nd * nh
        planes, rows = cx + 2 * XP, cy + 2 * YP
        f32 = jnp.float32
        block = pltpu.VMEM((cx, cy, cz), f32)
        dma = pltpu.SemaphoreType.DMA
        hbm = pl.BlockSpec(memory_space=pltpu.HBM)
        vmem = pl.BlockSpec(memory_space=pltpu.VMEM)
        between = (
            pltpu.VMEM((6, planes, rows, cz), f32),
            pltpu.VMEM((3, planes, rows, cz), f32),
            pltpu.VMEM((6, cx, cy, cz), f32),
            pltpu.VMEM((3, cx, cy, cz), f32),
            pltpu.VMEM((4, 4, cy, cz), f32),
            pltpu.VMEM((6 * cx, cz), f32),
        )
        held = pl.pallas_call(
            functools.partial(kernel, (ns, nd, nh, cx, cy, subf)),
            out_shape=between,
            in_specs=[hbm] * 12,
            out_specs=(vmem,) * 6,
            scratch_shapes=[
                block, block, block, block, block,
                pltpu.VMEM((6, rate.shape[1], 128), f32),
                pltpu.VMEM(cell.shape, jnp.int32),
                pltpu.SMEM(active.shape, jnp.int32),
                pltpu.SMEM(offset.shape, jnp.int32),
                pltpu.VMEM((4, 5, cx, cz), f32),
                pltpu.VMEM((4, 5, cx, cz), f32),
                pltpu.VMEM((4, 5, cx, cz), f32),
                pltpu.VMEM((4, 5, cx, cz), f32),
                pltpu.VMEM((4, 2, cy, cz), f32),
                pltpu.VMEM((4, 2, cy, cz), f32),
                pltpu.VMEM((4, 2, cy, cz), f32),
                pltpu.VMEM((2, 2 * cz, cz), jnp.bfloat16),
                pltpu.VMEM((ns // NA, STEPS, 8, 128), f32),
                pltpu.VMEM((NA, STEPS, 8, 128), f32),
                pltpu.VMEM((STEPS, 8, 128), f32),
                pltpu.VMEM((nd * nh, STEPS, 8, 128), f32),
                pltpu.VMEM((3 * 6 * cx, cz), f32),
                pltpu.VMEM((6 * cx, cz), f32),
                dma((20,)), dma((4, 4)), dma((4, 4)), dma((4, 2)), dma((4, 2)), dma((4, 2)), dma((4, 2)),
                dma((ns // NA,)), dma((ns // NA,)), dma, dma, dma((nh,)), dma((nd * nh,)),
            ],
            compiler_params=pltpu.CompilerParams(
                collective_id=0, has_side_effects=True, vmem_limit_bytes=40 * 1024 * 1024
            ),
            cost_estimate=pl.CostEstimate(flops=30_000_000, bytes_accessed=6_000_000, transcendentals=0),
        )(*(
            pltpu.with_memory_space_constraint(a, pltpu.HBM)
            for a in (velocity, stress, memory, lam, mu, buo, rel, ane, jnp.transpose(rate, (0, 2, 1, 3)), cell, active, offset)
        ))
        return pl.pallas_call(
            functools.partial(finish, (cx, cy)),
            out_shape=tuple(jax.ShapeDtypeStruct(a.shape, f32) for a in (velocity, stress, memory)),
            in_specs=[vmem] * 6,
            out_specs=(hbm,) * 3,
            scratch_shapes=[
                pltpu.VMEM((6, 4, cy, cz), f32),
                pltpu.VMEM((6, 4, cy, cz), f32),
                dma((7,)),
            ],
            compiler_params=pltpu.CompilerParams(vmem_limit_bytes=40 * 1024 * 1024),
            cost_estimate=pl.CostEstimate(flops=2_000_000, bytes_accessed=4_000_000, transcendentals=0),
        )(*held)

    field = P(None, "strike", "dip", "depth")
    cellwise = P("strike", "dip", "depth")
    return jax.shard_map(
        body,
        mesh=mesh,
        in_specs=(field,) * 3 + (cellwise,) * 5 + (P("strike", None, None, None), P(), P(), P()),
        out_specs=(field,) * 3,
        check_vma=False,
    )
```

profile of v0, /device:TPU:12, one launch (start us, length us, event | category | flops | bytes accessed | tf_op | source)
XLA Modules:
  0.0 38.9 jit_solution(6830591147935554086)
XLA Ops:
  0.6 36.3 %shard_map.139 = (f32[6,20,48,128]{3,2,1,0:T(8,128)S(1)}, f32[3,20,48,128]{3,2,1,0:T(8,128)S(1)}, f32[6,16,32,128]{3,2,1,0:T(8,128)S(1)}, f32[3,16,32,128]{3,2,1...) custom-call(f32[3,16,32,128]{3,2,1,0:T(8,128)} %vel_hbm.1, f32[6,16,32,128]{3,2,1,0:T(8,128)} %str_hbm.1, ...), custom_call_target="tpu_custom_call" | custom-call | flops 30000000 | bytes 6000000 | tf_op jit(solution)/shard_map/pallas_call | solution.py:639
  37.0 2.0 %shard_map.140 = (f32[3,16,32,128]{3,2,1,0:T(8,128)}, f32[6,16,32,128]{3,2,1,0:T(8,128)}, f32[6,16,32,128]{3,2,1,0:T(8,128)}) custom-call(f32[6,20,48,128]{3,2,1,0:T(8,128)S(1)} %get-tuple-element.9.S, f32[3,20,48,128]{3,2,1,0:T(8,128)S(1)} %get-tuple-element.10.V, f32[6,16,32,128]{3,2,1,0:T(8,128)S(1)} %get-tuple-element.11.M, ...), custom_call_target="tpu_custom_call" | custom-call | flops 2000000 | bytes 4000000 | tf_op jit(solution)/shard_map/pallas_call | solution.py:675
where the time goes:
time: 39.5 us; the launch traced here: 38.9 us
  Pallas kernels  38.3 us (97%)
  between operations  0.64 us (2%)
    pallas_call x1, Pallas kernels, body(): pl.pallas_call(functools.partial(kernel, (ns, nd, nh, cx, cy, subf)), out...  36.3 us
    pallas_call x1, Pallas kernels, body(): pl.pallas_call(functools.partial(finish, (cx, cy)), out_shape=tuple((jax....  1.97 us

commit v1 on v0

--- a/solution.py
+++ b/solution.py
@@ -21,9 +21,9 @@
 Z_BACK = {"s": (True, True, False), "v": (False, False, True)}
 
 
-def stress_tiles(x, m, sizes, Sf, Vf, M, deep, material, put):
+def stress_tiles(x, m, sizes, tiles, Sf, Vf, M, deep, material, put):
     CY, ROW = sizes
-    for j in range(0, CY, 8):
+    for j in tiles:
         at = (x + XP) * ROW + YP + j
         rows = pl.ds(j, 8)
 
@@ -86,7 +86,7 @@
             stress[c, place, rows, :] = s
             memory[c, place, rows, :] = m
 
-        stress_tiles(x, 2 * i, (CY, ROW), Sf, Vf, M, deep, material, put)
+        stress_tiles(x, 2 * i, (CY, ROW), range(0, CY, 8), Sf, Vf, M, deep, material, put)
 
     for c in range(6):
         for n, x in enumerate((0, 1, CX - 2, CX - 1)):
@@ -114,6 +114,7 @@
 ):
     NS, ND, NH, CX, CY, SUBF = dims
     ROW = CY + 2 * YP
+    HALF = CY // 2
     NB = NS // NA
     s = lax.axis_index("strike")
     k = lax.axis_index("dip")
@@ -158,7 +159,7 @@
         pltpu.make_async_copy(active_hbm, active, ld_sem.at[18]),
         pltpu.make_async_copy(offset_hbm, offset, ld_sem.at[19]),
     )
-    for copy in (loads[0], *order, *loads[1:]):
+    for copy in (loads[1], *order, loads[0], loads[2], loads[3]):
         copy.start()
 
     barrier = pltpu.get_barrier_semaphore()
@@ -210,25 +211,26 @@
     count = count + jnp.where(on_fault, ND * NH - 1, 0)
     pl.semaphore_wait(barrier, count)
 
-    def x_copies(h):
+    def x_copies(h, half):
         kind = "sv"[h % 2]
         ref = S if kind == "s" else V
         up, dn = [], []
         for n, (c0, nc, lu, ld) in enumerate(X_GROUPS[kind]):
             comps = pl.ds(c0, nc)
-            rows = pl.ds(YP, CY)
+            rows = pl.ds(YP + half * HALF, HALF)
             if h == 0:
-                src_up = str_hbm.at[comps, pl.ds(CX - lu, lu)]
-                src_dn = str_hbm.at[comps, pl.ds(0, ld)]
+                whole = pl.ds(half * HALF, HALF)
+                src_up = str_hbm.at[comps, pl.ds(CX - lu, lu), whole]
+                src_dn = str_hbm.at[comps, pl.ds(0, ld), whole]
             else:
                 src_up = ref.at[comps, pl.ds(XP + CX - lu, lu), rows]
                 src_dn = ref.at[comps, pl.ds(XP, ld), rows]
             up.append(pltpu.make_async_remote_copy(
                 src_up, ref.at[comps, pl.ds(XP - lu, lu), rows],
-                xs_sem.at[h, n], xr_sem.at[h, n], device_id=s_up, device_id_type=MESH))
+                xs_sem.at[h, half, n], xr_sem.at[h, half, n], device_id=s_up, device_id_type=MESH))
             dn.append(pltpu.make_async_remote_copy(
                 src_dn, ref.at[comps, pl.ds(XP + CX, ld), rows],
-                xs_sem.at[h, 2 + n], xr_sem.at[h, 2 + n], device_id=s_dn, device_id_type=MESH))
+                xs_sem.at[h, half, 2 + n], xr_sem.at[h, half, 2 + n], device_id=s_dn, device_id_type=MESH))
         return up, dn
 
     def each(there, copies, act):
@@ -237,22 +239,24 @@
             for copy in copies:
                 act(copy)
 
-    def x_start(h):
-        up, dn = x_copies(h)
+    def x_start(h, half):
+        up, dn = x_copies(h, half)
         each(has["s_up"], up, lambda c: c.start())
         each(has["s_dn"], dn, lambda c: c.start())
 
-    def x_wait_recv(h):
-        up, dn = x_copies(h)
+    def x_wait_recv(h, half):
+        up, dn = x_copies(h, half)
         each(has["s_dn"], up, lambda c: c.wait_recv())
         each(has["s_up"], dn, lambda c: c.wait_recv())
 
     def x_wait_send(h):
-        up, dn = x_copies(h)
-        each(has["s_up"], up, lambda c: c.wait_send())
-        each(has["s_dn"], dn, lambda c: c.wait_send())
-
-    x_start(0)
+        for half in range(2):
+            up, dn = x_copies(h, half)
+            each(has["s_up"], up, lambda c: c.wait_send())
+            each(has["s_dn"], dn, lambda c: c.wait_send())
+
+    x_start(0, 0)
+    x_start(0, 1)
 
     Sf = S.reshape(6, (CX + 2 * XP) * ROW, 128)
     Vf = V.reshape(3, (CX + 2 * XP) * ROW, 128)
@@ -382,8 +386,8 @@
                 (((1,), (0,)), ((), ())), preferred_element_type=jnp.float32)
             deep[place] = out.reshape(CX, CY, 128)
 
-    def velocity_pair(x):
-        for j in range(0, CY, 8):
+    def velocity_pair(x, tiles):
+        for j in tiles:
             at = (x + XP) * ROW + YP + j
 
             def get(c, n, Sf=Sf, at=at):
@@ -411,7 +415,7 @@
                     Vf[c, own, :] = Vf[c, own, :] + gain * (
                         27.0 * close[c] - far[c] + deep[c, x + p, pl.ds(j, 8), :])
 
-    def stress_pair(x):
+    def stress_pair(x, tiles):
         def material(x, rows):
             return lam[x, rows, :], mu[x, rows, :], rel[x, rows, :], ane[x, rows, :]
 
@@ -419,17 +423,17 @@
             Sf[c, pl.ds(pl.multiple_of(at, 8), 8), :] = stress
             M[c, x, rows, :] = memory
 
-        stress_tiles(x, x, (CY, ROW), Sf, Vf, M, deep, material, put)
+        stress_tiles(x, x, (CY, ROW), tiles, Sf, Vf, M, deep, material, put)
 
     def interior(one):
         @pl.loop(0, (CX - 4) // 2)
         def _(i):
-            one(2 * i + 2)
-
-    def boundary(one):
+            one(2 * i + 2, range(0, CY, 8))
+
+    def boundary(one, half):
         @pl.loop(0, 2)
         def _(i):
-            one(i * (CX - 2))
+            one(i * (CX - 2), range(half * HALF, (half + 1) * HALF, 8))
 
     def candidates():
         row = lax.broadcasted_iota(jnp.int32, (TB, 128), 0)
@@ -558,48 +562,55 @@
     def _():
         last_plane[...] = jnp.zeros_like(last_plane)
 
+    source_first()
     loads[0].wait()
+    for copy in loads[4:]:
+        copy.start()
     yz_send(0)
-    source_first()
     deep_all(0)
+    source_second()
     loads[2].wait()
     loads[3].wait()
     yz_recv(0)
     interior(velocity_pair)
-    source_second()
-    x_wait_recv(0)
-    boundary(velocity_pair)
-    x_start(1)
+    source_third()
+    for half in range(2):
+        x_wait_recv(0, half)
+        boundary(velocity_pair, half)
+        x_start(1, half)
     yz_send(1)
-    source_third()
     deep_all(1)
     for copy in loads[4:]:
         copy.wait()
+    source_gather()
+    source_plane(0)
     yz_recv(1)
     interior(stress_pair)
-    source_gather()
-    source_plane(0)
     apply_source(plane, middle)
-    x_wait_recv(1)
     x_wait_send(0)
-    boundary(stress_pair)
-    apply_source(plane, edges)
-    x_start(2)
+    for half in range(2):
+        x_wait_recv(1, half)
+        boundary(stress_pair, half)
+        if half == 0:
+            apply_source(plane, edges)
+        x_start(2, half)
     yz_send(2)
     deep_all(2)
     source_plane(1)
     x_wait_send(1)
     yz_recv(2)
     interior(velocity_pair)
-    x_wait_recv(2)
-    boundary(velocity_pair)
-    x_start(3)
+    for half in range(2):
+        x_wait_recv(2, half)
+        boundary(velocity_pair, half)
+        x_start(3, half)
     yz_send(3)
     deep_all(3)
     yz_recv(3)
     interior(stress_pair)
     apply_source(last_plane, middle)
-    x_wait_recv(3)
+    for half in range(2):
+        x_wait_recv(3, half)
 
     x_wait_send(2)
     x_wait_send(3)
@@ -661,7 +672,7 @@
                 pltpu.VMEM((nd * nh, STEPS, 8, 128), f32),
                 pltpu.VMEM((3 * 6 * cx, cz), f32),
                 pltpu.VMEM((6 * cx, cz), f32),
-                dma((20,)), dma((4, 4)), dma((4, 4)), dma((4, 2)), dma((4, 2)), dma((4, 2)), dma((4, 2)),
+                dma((20,)), dma((4, 2, 4)), dma((4, 2, 4)), dma((4, 2)), dma((4, 2)), dma((4, 2)), dma((4, 2)),
                 dma((ns // NA,)), dma((ns // NA,)), dma, dma, dma((nh,)), dma((nd * nh,)),
             ],
             compiler_params=pltpu.CompilerParams(

time: 39.5 us -> 40.8 us (1.033); the launches traced: 38.9 us -> 40.7 us
  Pallas kernels: 38.3 us -> 40 us
    pallas_call x1, Pallas kernels: 36.3 us -> 38.1 us  [body(): pl.pallas_call(functools.partial(kernel, (ns, nd, nh, cx, cy, subf)), out...]
where the time goes in v1:
time: 40.8 us; the launch traced here: 40.7 us
  Pallas kernels  40 us (98%)
  between operations  0.64 us (2%)
    pallas_call x1, Pallas kernels, body(): pl.pallas_call(functools.partial(kernel, (ns, nd, nh, cx, cy, subf)), out...  38.1 us
    pallas_call x1, Pallas kernels, body(): pl.pallas_call(functools.partial(finish, (cx, cy)), out_shape=tuple((jax....  1.97 us

profile of v1, /device:TPU:12, one launch (start us, length us, event | category | flops | bytes accessed | tf_op | source)
XLA Modules:
  0.0 40.7 jit_solution(5014520150952832828)
XLA Ops:
  0.6 38.1 %shard_map.139 = (f32[6,20,48,128]{3,2,1,0:T(8,128)S(1)}, f32[3,20,48,128]{3,2,1,0:T(8,128)S(1)}, f32[6,16,32,128]{3,2,1,0:T(8,128)S(1)}, f32[3,16,32,128]{3,2,1...) custom-call(f32[3,16,32,128]{3,2,1,0:T(8,128)} %vel_hbm.1, f32[6,16,32,128]{3,2,1,0:T(8,128)} %str_hbm.1, ...), custom_call_target="tpu_custom_call" | custom-call | flops 30000000 | bytes 6000000 | tf_op jit(solution)/shard_map/pallas_call | solution.py:650
  38.7 2.0 %shard_map.140 = (f32[3,16,32,128]{3,2,1,0:T(8,128)}, f32[6,16,32,128]{3,2,1,0:T(8,128)}, f32[6,16,32,128]{3,2,1,0:T(8,128)}) custom-call(f32[6,20,48,128]{3,2,1,0:T(8,128)S(1)} %get-tuple-element.9.S, f32[3,20,48,128]{3,2,1,0:T(8,128)S(1)} %get-tuple-element.10.V, f32[6,16,32,128]{3,2,1,0:T(8,128)S(1)} %get-tuple-element.11.M, ...), custom_call_target="tpu_custom_call" | custom-call | flops 2000000 | bytes 4000000 | tf_op jit(solution)/shard_map/pallas_call | solution.py:686

commit v2 on v0

--- a/solution.py
+++ b/solution.py
@@ -21,9 +21,9 @@
 Z_BACK = {"s": (True, True, False), "v": (False, False, True)}
 
 
-def stress_tiles(x, m, sizes, Sf, Vf, M, deep, material, put):
+def stress_tiles(x, m, sizes, tiles, Sf, Vf, M, deep, material, put):
     CY, ROW = sizes
-    for j in range(0, CY, 8):
+    for j in tiles:
         at = (x + XP) * ROW + YP + j
         rows = pl.ds(j, 8)
 
@@ -59,7 +59,7 @@
                 put(c, x + p, at + o, rows, stress, new)
 
 
-def finish(dims, S, V, M, deep, edge, plane, vel_out, str_out, mem_out, stress, memory, sem):
+def finish(dims, S, V, M, deep, lam, mu, rel, ane, plane, vel_out, str_out, mem_out, stress, memory, sem):
     CX, CY = dims
     ROW = CY + 2 * YP
     own = pl.ds(YP, CY)
@@ -79,14 +79,14 @@
         x = i * (CX - 2)
 
         def material(m, rows):
-            return tuple(edge[n, m, rows, :] for n in range(4))
+            return tuple(ref[m, rows, :] for ref in (lam, mu, rel, ane))
 
         def put(c, at_x, at, rows, s, m):
             place = at_x - i * (CX - 4)
             stress[c, place, rows, :] = s
             memory[c, place, rows, :] = m
 
-        stress_tiles(x, 2 * i, (CY, ROW), Sf, Vf, M, deep, material, put)
+        stress_tiles(x, x, (CY, ROW), range(0, CY, 8), Sf, Vf, M, deep, material, put)
 
     for c in range(6):
         for n, x in enumerate((0, 1, CX - 2, CX - 1)):
@@ -105,8 +105,8 @@
     dims,
     vel_hbm, str_hbm, mem_hbm, lam_hbm, mu_hbm, buo_hbm, rel_hbm, ane_hbm, rate_hbm, cell_hbm,
     active_hbm, offset_hbm,
-    S, V, M, deep, edge, last_plane,
-    lam, mu, buo, rel, ane, rate, cells, active, offset,
+    S, V, M, deep, lam, mu, rel, ane, last_plane,
+    buo, rate, cells, active, offset,
     ysend_up, ysend_dn, yrecv_up, yrecv_dn, zsend, zrecv_up, zrecv_dn, band,
     cand, pair, chosen, gathered, acc, plane,
     ld_sem, xs_sem, xr_sem, ys_sem, yr_sem, zs_sem, zr_sem,
@@ -150,15 +150,11 @@
         pltpu.make_async_copy(ane_hbm, ane, ld_sem.at[8]),
         pltpu.make_async_copy(cell_hbm, cells, ld_sem.at[9]),
     ]
-    for n, ref in enumerate((lam_hbm, mu_hbm, rel_hbm, ane_hbm)):
-        for m in range(2):
-            loads.append(pltpu.make_async_copy(
-                ref.at[pl.ds(m * (CX - 2), 2)], edge.at[n, pl.ds(2 * m, 2)], ld_sem.at[10 + 2 * n + m]))
     order = (
-        pltpu.make_async_copy(active_hbm, active, ld_sem.at[18]),
-        pltpu.make_async_copy(offset_hbm, offset, ld_sem.at[19]),
+        pltpu.make_async_copy(active_hbm, active, ld_sem.at[10]),
+        pltpu.make_async_copy(offset_hbm, offset, ld_sem.at[11]),
     )
-    for copy in (loads[0], *order, *loads[1:]):
+    for copy in (loads[1], *order, loads[0], loads[2], loads[3]):
         copy.start()
 
     barrier = pltpu.get_barrier_semaphore()
@@ -269,15 +265,17 @@
         def _(F=F, zero_x=zero_x):
             F[:, XP + CX:, YP:YP + CY, :] = zero_x
 
-    zero_y = jnp.zeros(yrecv_up.shape, jnp.float32)
-    zero_z = jnp.zeros(zrecv_up.shape, jnp.float32)
-    for there, ref, zero in (
-        (has["k_dn"], yrecv_up, zero_y), (has["k_up"], yrecv_dn, zero_y),
-        (has["d_dn"], zrecv_up, zero_z), (has["d_up"], zrecv_dn, zero_z),
+    for there, refs in (
+        (has["k_dn"], yrecv_up), (has["k_up"], yrecv_dn), (has["d_dn"], zrecv_up), (has["d_up"], zrecv_dn),
     ):
         @pl.when(jnp.logical_not(there))
-        def _(ref=ref, zero=zero):
-            ref[...] = zero
+        def _(refs=refs):
+            for ref in refs:
+                ref[...] = jnp.zeros(ref.shape, jnp.float32)
+
+    for refs in (ysend_up, ysend_dn):
+        for ref in refs:
+            ref[:, ref.shape[1] - 8:, :] = jnp.zeros((4, 8, 128), jnp.float32)
 
     def y_layers(kind):
         up, dn = [], []
@@ -286,26 +284,29 @@
             dn += [(c, 0)] if back else [(c, 0), (c, 1)]
         return up, dn
 
-    def y_copies(h):
-        up, dn = y_layers("sv"[h % 2])
-        nu, nd = len(up), len(dn)
+    PLANES = (tuple(range(2, CX - 2)), (0, 1, CX - 2, CX - 1))
+    SPANS = (((2, CX - 4),), ((0, 2), (CX - 2, 2)))
+
+    def y_copies(h, part):
+        size = len(PLANES[part])
+        nu, nd = (-(-len(layers) * size // 8) * 8 for layers in y_layers("sv"[h % 2]))
         return (
             pltpu.make_async_remote_copy(
-                ysend_up.at[h, pl.ds(0, nu)], yrecv_up.at[h, pl.ds(0, nu)],
-                ys_sem.at[h, 0], yr_sem.at[h, 0], device_id=k_up, device_id_type=MESH),
+                ysend_up[part].at[h, pl.ds(0, nu)], yrecv_up[part].at[h, pl.ds(0, nu)],
+                ys_sem.at[h, part, 0], yr_sem.at[h, part, 0], device_id=k_up, device_id_type=MESH),
             pltpu.make_async_remote_copy(
-                ysend_dn.at[h, pl.ds(0, nd)], yrecv_dn.at[h, pl.ds(0, nd)],
-                ys_sem.at[h, 1], yr_sem.at[h, 1], device_id=k_dn, device_id_type=MESH),
+                ysend_dn[part].at[h, pl.ds(0, nd)], yrecv_dn[part].at[h, pl.ds(0, nd)],
+                ys_sem.at[h, part, 1], yr_sem.at[h, part, 1], device_id=k_dn, device_id_type=MESH),
         )
 
-    def z_copies(h):
+    def z_copies(h, part):
         return (
             pltpu.make_async_remote_copy(
-                zsend.at[h], zrecv_up.at[h],
-                zs_sem.at[h, 0], zr_sem.at[h, 0], device_id=d_up, device_id_type=MESH),
+                zsend[part].at[h], zrecv_up[part].at[h],
+                zs_sem.at[h, part, 0], zr_sem.at[h, part, 0], device_id=d_up, device_id_type=MESH),
             pltpu.make_async_remote_copy(
-                zsend.at[h], zrecv_dn.at[h],
-                zs_sem.at[h, 1], zr_sem.at[h, 1], device_id=d_dn, device_id_type=MESH),
+                zsend[part].at[h], zrecv_dn[part].at[h],
+                zs_sem.at[h, part, 1], zr_sem.at[h, part, 1], device_id=d_dn, device_id_type=MESH),
         )
 
     lane = lax.broadcasted_iota(jnp.int32, (CY, 128), 1)
@@ -315,75 +316,86 @@
     def turn(value, n):
         return pltpu.roll(value, n % 128, 1)
 
-    def yz_send(h):
+    def z_slot(part, place, n):
+        if part == 0:
+            return place // 2, n + 16 * (place % 2)
+        return 0, n + 4 * place
+
+    def yz_send(h, part):
         kind = "sv"[h % 2]
         F = flat[kind]
-        up, dn = y_layers(kind)
         base = XP * ROW + YP
-        for n, (c, row) in enumerate(up):
-            ysend_up[h, n] = F[c, pl.ds(base + row, CX, stride=ROW), :]
-        for n, (c, row) in enumerate(dn):
-            ysend_dn[h, n] = F[c, pl.ds(base + row, CX, stride=ROW), :]
-        up, dn = y_copies(h)
+        for layers, refs in zip(y_layers(kind), (ysend_up, ysend_dn)):
+            at = 0
+            for c, row in layers:
+                for x0, n in SPANS[part]:
+                    refs[part][h, at:at + n, :] = F[c, pl.ds(base + x0 * ROW + row, n, stride=ROW), :]
+                    at += n
+        up, dn = y_copies(h, part)
         each(has["k_up"], [up], lambda c: c.start())
         each(has["k_dn"], [dn], lambda c: c.start())
-
-        first = second = jnp.zeros((CY, 128), jnp.float32)
-        for x in range(CX):
-            a, b, c = (F[comp, pl.ds((x + XP) * ROW + YP, CY), :] for comp in Z_FIELDS[kind])
-            first = jnp.where(slot == x, turn(a, 4 * x + 2), first)
-            first = jnp.where(slot == x + CX, turn(b, 4 * x + 66), first)
-            second = jnp.where(slot == x, turn(c, 4 * x + 2), second)
-        zsend[h, 0] = first
-        zsend[h, 1] = second
-        up, dn = z_copies(h)
+        arrays = [jnp.zeros((CY, 128), jnp.float32)] * (2 - part)
+        for place, comp in enumerate(Z_FIELDS[kind]):
+            for n, x in enumerate(PLANES[part]):
+                where, index = z_slot(part, place, n)
+                value = F[comp, pl.ds((x + XP) * ROW + YP, CY), :]
+                arrays[where] = jnp.where(slot == index, turn(value, 4 * index + 2), arrays[where])
+        for n, value in enumerate(arrays):
+            zsend[part][h, n] = value
+        up, dn = z_copies(h, part)
         each(has["d_up"], [up], lambda c: c.start())
         each(has["d_dn"], [dn], lambda c: c.start())
 
-    def yz_recv(h):
+    def yz_recv(h, part):
         kind = "sv"[h % 2]
         F = flat[kind]
-        up, dn = y_copies(h)
+        up, dn = y_copies(h, part)
         each(has["k_dn"], [up], lambda c: c.wait_recv())
         each(has["k_up"], [dn], lambda c: c.wait_recv())
-        up, dn = y_layers(kind)
         base = XP * ROW + YP
-        for n, (c, row) in enumerate(up):
-            F[c, pl.ds(base + row - CY, CX, stride=ROW), :] = yrecv_up[h, n]
-        for n, (c, row) in enumerate(dn):
-            F[c, pl.ds(base + row + CY, CX, stride=ROW), :] = yrecv_dn[h, n]
-        up, dn = z_copies(h)
+        for layers, refs, shift in zip(y_layers(kind), (yrecv_up, yrecv_dn), (-CY, CY)):
+            at = 0
+            for c, row in layers:
+                for x0, n in SPANS[part]:
+                    F[c, pl.ds(base + x0 * ROW + row + shift, n, stride=ROW), :] = refs[part][h, at:at + n, :]
+                    at += n
+        up, dn = z_copies(h, part)
         each(has["d_dn"], [up], lambda c: c.wait_recv())
         each(has["d_up"], [dn], lambda c: c.wait_recv())
-        fixes = []
-        for n in range(2):
-            mix = jnp.where(quarter < 2, zrecv_up[h, n], zrecv_dn[h, n])
-            below, two_after = turn(mix, 1), turn(mix, -2)
-            if Z_BACK[kind][2 * n]:
-                fix = jnp.where(quarter == 0, -two_after, jnp.where(quarter == 1, below - 27.0 * mix, below))
-            else:
-                fix = jnp.where(quarter == 1, 27.0 * turn(mix, -1) - two_after, jnp.where(quarter == 0, -two_after, below))
-            fixes.append(jnp.where(quarter == 3, 0.0, fix))
+        fixes = {}
         for place, back in enumerate(Z_BACK[kind]):
             ends = (lane == 127) | (lane < 2) if back else (lane > 125) | (lane == 0)
-            for x in range(CX):
-                moved = turn(fixes[place // 2], (127 if back else 126) - 4 * x - 64 * (place % 2))
+            for n, x in enumerate(PLANES[part]):
+                where, index = z_slot(part, place, n)
+                if (where, back) not in fixes:
+                    mix = jnp.where(quarter < 2, zrecv_up[part][h, where], zrecv_dn[part][h, where])
+                    below, two_after = turn(mix, 1), turn(mix, -2)
+                    if back:
+                        fix = jnp.where(quarter == 0, -two_after, jnp.where(quarter == 1, below - 27.0 * mix, below))
+                    else:
+                        fix = jnp.where(quarter == 1, 27.0 * turn(mix, -1) - two_after, jnp.where(quarter == 0, -two_after, below))
+                    fixes[where, back] = jnp.where(quarter == 3, 0.0, fix)
+                moved = turn(fixes[where, back], (127 if back else 126) - 4 * index)
                 deep[place, x] = deep[place, x] + jnp.where(ends, moved, 0.0)
 
-    def deep_all(h):
+    def deep_part(h, part):
         kind = "sv"[h % 2]
         F = S if kind == "s" else V
         for place, (comp, back) in enumerate(zip(Z_FIELDS[kind], Z_BACK[kind])):
-            f = F[comp, XP:XP + CX, YP:YP + CY, :].reshape(CX * CY, 128)
+            f = jnp.concatenate(
+                [F[comp, XP + x0:XP + x0 + n, YP:YP + CY, :].reshape(n * CY, 128) for x0, n in SPANS[part]], axis=0)
             high = f.astype(jnp.bfloat16)
             low = (f - high.astype(jnp.float32)).astype(jnp.bfloat16)
             out = lax.dot_general(
                 jnp.concatenate([high, low], axis=1), band[1 if back else 0],
                 (((1,), (0,)), ((), ())), preferred_element_type=jnp.float32)
-            deep[place] = out.reshape(CX, CY, 128)
-
-    def velocity_pair(x):
-        for j in range(0, CY, 8):
+            at = 0
+            for x0, n in SPANS[part]:
+                deep[place, x0:x0 + n] = out[at:at + n * CY].reshape(n, CY, 128)
+                at += n * CY
+
+    def velocity_pair(x, tiles):
+        for j in tiles:
             at = (x + XP) * ROW + YP + j
 
             def get(c, n, Sf=Sf, at=at):
@@ -411,7 +423,7 @@
                     Vf[c, own, :] = Vf[c, own, :] + gain * (
                         27.0 * close[c] - far[c] + deep[c, x + p, pl.ds(j, 8), :])
 
-    def stress_pair(x):
+    def stress_pair(x, tiles):
         def material(x, rows):
             return lam[x, rows, :], mu[x, rows, :], rel[x, rows, :], ane[x, rows, :]
 
@@ -419,17 +431,17 @@
             Sf[c, pl.ds(pl.multiple_of(at, 8), 8), :] = stress
             M[c, x, rows, :] = memory
 
-        stress_tiles(x, x, (CY, ROW), Sf, Vf, M, deep, material, put)
+        stress_tiles(x, x, (CY, ROW), tiles, Sf, Vf, M, deep, material, put)
 
     def interior(one):
         @pl.loop(0, (CX - 4) // 2)
         def _(i):
-            one(2 * i + 2)
+            one(2 * i + 2, range(0, CY, 8))
 
     def boundary(one):
         @pl.loop(0, 2)
         def _(i):
-            one(i * (CX - 2))
+            one(i * (CX - 2), range(0, CY, 8))
 
     def candidates():
         row = lax.broadcasted_iota(jnp.int32, (TB, 128), 0)
@@ -558,58 +570,70 @@
     def _():
         last_plane[...] = jnp.zeros_like(last_plane)
 
+    source_first()
     loads[0].wait()
-    yz_send(0)
-    source_first()
-    deep_all(0)
+    for copy in loads[4:]:
+        copy.start()
+    yz_send(0, 0)
+    yz_send(0, 1)
+    deep_part(0, 0)
+    deep_part(0, 1)
     loads[2].wait()
     loads[3].wait()
-    yz_recv(0)
+    yz_recv(0, 0)
+    source_second()
     interior(velocity_pair)
-    source_second()
+    yz_send(1, 0)
+    source_third()
+    deep_part(1, 0)
+    yz_recv(0, 1)
     x_wait_recv(0)
     boundary(velocity_pair)
     x_start(1)
-    yz_send(1)
-    source_third()
-    deep_all(1)
+    yz_send(1, 1)
     for copy in loads[4:]:
         copy.wait()
-    yz_recv(1)
+    yz_recv(1, 0)
     interior(stress_pair)
     source_gather()
     source_plane(0)
     apply_source(plane, middle)
+    yz_send(2, 0)
+    deep_part(1, 1)
+    deep_part(2, 0)
+    x_wait_send(0)
+    yz_recv(1, 1)
     x_wait_recv(1)
-    x_wait_send(0)
     boundary(stress_pair)
     apply_source(plane, edges)
     x_start(2)
-    yz_send(2)
-    deep_all(2)
+    yz_send(2, 1)
+    yz_recv(2, 0)
+    interior(velocity_pair)
+    yz_send(3, 0)
+    deep_part(2, 1)
+    deep_part(3, 0)
     source_plane(1)
     x_wait_send(1)
-    yz_recv(2)
-    interior(velocity_pair)
+    yz_recv(2, 1)
     x_wait_recv(2)
     boundary(velocity_pair)
     x_start(3)
-    yz_send(3)
-    deep_all(3)
-    yz_recv(3)
+    yz_send(3, 1)
+    yz_recv(3, 0)
     interior(stress_pair)
     apply_source(last_plane, middle)
+    deep_part(3, 1)
+    yz_recv(3, 1)
     x_wait_recv(3)
 
     x_wait_send(2)
     x_wait_send(3)
     for h in range(4):
-        up, dn = y_copies(h)
-        each(has["k_up"], [up], lambda c: c.wait_send())
-        each(has["k_dn"], [dn], lambda c: c.wait_send())
-        up, dn = z_copies(h)
-        each(has["d_up"], [up], lambda c: c.wait_send())
-        each(has["d_dn"], [dn], lambda c: c.wait_send())
+        for part in range(2):
+            for there, pair_of in (("k", y_copies(h, part)), ("d", z_copies(h, part))):
+                each(has[there + "_up"], [pair_of[0]], lambda c: c.wait_send())
+                each(has[there + "_dn"], [pair_of[1]], lambda c: c.wait_send())
     over_groups(lambda g: c_copy(group, g).wait_send())
     pair_copy(parity).wait_send()
     over_fault(lambda h: g_copy(chunk, h).wait_send())
@@ -633,27 +657,22 @@
             pltpu.VMEM((3, planes, rows, cz), f32),
             pltpu.VMEM((6, cx, cy, cz), f32),
             pltpu.VMEM((3, cx, cy, cz), f32),
-            pltpu.VMEM((4, 4, cy, cz), f32),
+            block, block, block, block,
             pltpu.VMEM((6 * cx, cz), f32),
         )
         held = pl.pallas_call(
             functools.partial(kernel, (ns, nd, nh, cx, cy, subf)),
             out_shape=between,
             in_specs=[hbm] * 12,
-            out_specs=(vmem,) * 6,
+            out_specs=(vmem,) * 9,
             scratch_shapes=[
-                block, block, block, block, block,
+                block,
                 pltpu.VMEM((6, rate.shape[1], 128), f32),
                 pltpu.VMEM(cell.shape, jnp.int32),
                 pltpu.SMEM(active.shape, jnp.int32),
                 pltpu.SMEM(offset.shape, jnp.int32),
-                pltpu.VMEM((4, 5, cx, cz), f32),
-                pltpu.VMEM((4, 5, cx, cz), f32),
-                pltpu.VMEM((4, 5, cx, cz), f32),
-                pltpu.VMEM((4, 5, cx, cz), f32),
-                pltpu.VMEM((4, 2, cy, cz), f32),
-                pltpu.VMEM((4, 2, cy, cz), f32),
-                pltpu.VMEM((4, 2, cy, cz), f32),
+                *[(pltpu.VMEM((4, 64, cz), f32), pltpu.VMEM((4, 24, cz), f32))] * 4,
+                *[(pltpu.VMEM((4, 2, cy, cz), f32), pltpu.VMEM((4, 1, cy, cz), f32))] * 3,
                 pltpu.VMEM((2, 2 * cz, cz), jnp.bfloat16),
                 pltpu.VMEM((ns // NA, STEPS, 8, 128), f32),
                 pltpu.VMEM((NA, STEPS, 8, 128), f32),
@@ -661,7 +680,7 @@
                 pltpu.VMEM((nd * nh, STEPS, 8, 128), f32),
                 pltpu.VMEM((3 * 6 * cx, cz), f32),
                 pltpu.VMEM((6 * cx, cz), f32),
-                dma((20,)), dma((4, 4)), dma((4, 4)), dma((4, 2)), dma((4, 2)), dma((4, 2)), dma((4, 2)),
+                dma((12,)), dma((4, 4)), dma((4, 4)), dma((4, 2, 2)), dma((4, 2, 2)), dma((4, 2, 2)), dma((4, 2, 2)),
                 dma((ns // NA,)), dma((ns // NA,)), dma, dma, dma((nh,)), dma((nd * nh,)),
             ],
             compiler_params=pltpu.CompilerParams(
@@ -675,7 +694,7 @@
         return pl.pallas_call(
             functools.partial(finish, (cx, cy)),
             out_shape=tuple(jax.ShapeDtypeStruct(a.shape, f32) for a in (velocity, stress, memory)),
-            in_specs=[vmem] * 6,
+            in_specs=[vmem] * 9,
             out_specs=(hbm,) * 3,
             scratch_shapes=[
                 pltpu.VMEM((6, 4, cy, cz), f32),

time: 39.5 us -> 39.9 us (1.010); the launches traced: 38.9 us -> 39.9 us
  Pallas kernels: 38.3 us -> 39.2 us
    pallas_call x1, Pallas kernels: 36.3 us -> 37.2 us  [body(): pl.pallas_call(functools.partial(kernel, (ns, nd, nh, cx, cy, subf)), out...]
where the time goes in v2:
time: 39.9 us
  Pallas kernels  39.2 us (98%)
  between operations  0.64 us (2%)
    pallas_call x1, Pallas kernels, body(): pl.pallas_call(functools.partial(kernel, (ns, nd, nh, cx, cy, subf)), out...  37.2 us
    pallas_call x1, Pallas kernels, body(): pl.pallas_call(functools.partial(finish, (cx, cy)), out_shape=tuple((jax....  1.97 us

profile of v2, /device:TPU:12, one launch (start us, length us, event | category | flops | bytes accessed | tf_op | source)
XLA Modules:
  0.0 39.9 jit_solution(9590284692459292061)
XLA Ops:
  0.6 37.2 %shard_map.139 = (f32[6,20,48,128]{3,2,1,0:T(8,128)S(1)}, f32[3,20,48,128]{3,2,1,0:T(8,128)S(1)}, f32[6,16,32,128]{3,2,1,0:T(8,128)S(1)}, f32[3,16,32,128]{3,2,1...) custom-call(f32[3,16,32,128]{3,2,1,0:T(8,128)} %vel_hbm.1, ...), custom_call_target="tpu_custom_call" | custom-call | flops 30000000 | bytes 6000000 | tf_op jit(solution)/shard_map/pallas_call | solution.py:663
  37.9 2.0 %shard_map.140 = (f32[3,16,32,128]{3,2,1,0:T(8,128)}, f32[6,16,32,128]{3,2,1,0:T(8,128)}, f32[6,16,32,128]{3,2,1,0:T(8,128)}) custom-call(f32[6,20,48,128]{3,2,1,0:T(8,128)S(1)} %get-tuple-element.12.S, f32[3,20,48,128]{3,2,1,0:T(8,128)S(1)} %get-tuple-element.13.V, f32[6,16,32,128]{3,2,1,0:T(8,128)S(1)} %get-tuple-element.14.M, ...), custom_call_target="tpu_custom_call" | custom-call | flops 2000000 | bytes 4000000 | tf_op jit(solution)/shard_map/pallas_call | solution.py:694

commit v3 on v2

--- a/solution.py
+++ b/solution.py
@@ -14,6 +14,7 @@
 XP = 2
 YP = 8
 NA = 2
+CORES = 2
 
 X_GROUPS = {"s": ((0, 1, 1, 2), (3, 2, 2, 1)), "v": ((0, 1, 2, 1), (1, 2, 1, 2))}
 Y_FIELDS = {"s": ((3, True), (5, True), (1, False)), "v": ((1, True), (0, False), (2, False))}
@@ -108,8 +109,8 @@
     S, V, M, deep, lam, mu, rel, ane, last_plane,
     buo, rate, cells, active, offset,
     ysend_up, ysend_dn, yrecv_up, yrecv_dn, zsend, zrecv_up, zrecv_dn, band,
-    cand, pair, chosen, gathered, acc, plane,
-    ld_sem, xs_sem, xr_sem, ys_sem, yr_sem, zs_sem, zr_sem,
+    relay_0, relay_1, cand, pair, chosen, gathered, acc, plane,
+    fs_sem, fr_sem, ld_sem, xs_sem, xr_sem, ys_sem, yr_sem, zs_sem, zr_sem,
     c_send, c_recv, p_send, p_recv, g_send, g_recv,
 ):
     NS, ND, NH, CX, CY, SUBF = dims
@@ -133,6 +134,22 @@
         "s_up": s < NS - 1, "s_dn": s > 0,
         "k_up": k < ND - 1, "k_dn": k > 0,
         "d_up": d < NH - 1, "d_dn": d > 0,
+    }
+
+    low_chip = lax.div(d, CORES) == 0
+    even = parity == 0
+    via = {
+        "strike": jnp.where(low_chip, s, jnp.where(even, jnp.minimum(s + 1, NS - 1), jnp.maximum(s - 1, 0))),
+        "depth": jnp.where(low_chip, d + CORES, d - CORES),
+    }
+    from_s = jnp.where(low_chip, jnp.where(even, jnp.minimum(s + 1, NS - 1), jnp.maximum(s - 1, 0)), s)
+    from_d = jnp.where(low_chip, d + CORES, d - CORES)
+    forwards = from_s < NS - 1
+    sender = {"strike": from_s, "depth": from_d}
+    onward = {"strike": jnp.minimum(from_s + 1, NS - 1), "depth": from_d}
+    came_by = {
+        "strike": jnp.maximum(jnp.where(low_chip, s - 1, jnp.where(even, s - 2, s)), 0),
+        "depth": jnp.where(low_chip, d + CORES, d - CORES),
     }
 
     inner = (slice(None), pl.ds(XP, CX), pl.ds(YP, CY))
@@ -167,6 +184,16 @@
         def _(to=to):
             pl.semaphore_signal(barrier, inc=1, device_id=to, device_id_type=MESH)
 
+    count = count + has["s_up"].astype(jnp.int32) + forwards.astype(jnp.int32)
+
+    @pl.when(forwards)
+    def _():
+        pl.semaphore_signal(barrier, inc=1, device_id=sender, device_id_type=MESH)
+
+    @pl.when(has["s_dn"])
+    def _():
+        pl.semaphore_signal(barrier, inc=1, device_id=came_by, device_id_type=MESH)
+
     other = {"strike": group * NA + lax.rem(parity + 1, NA)}
     pl.semaphore_signal(barrier, inc=1, device_id=other, device_id_type=MESH)
     count = count + 1
@@ -206,10 +233,12 @@
     count = count + jnp.where(on_fault, ND * NH - 1, 0)
     pl.semaphore_wait(barrier, count)
 
+    relays = (relay_0, relay_1)
+
     def x_copies(h):
         kind = "sv"[h % 2]
         ref = S if kind == "s" else V
-        up, dn = [], []
+        up, dn, on = [], [], []
         for n, (c0, nc, lu, ld) in enumerate(X_GROUPS[kind]):
             comps = pl.ds(c0, nc)
             rows = pl.ds(YP, CY)
@@ -219,13 +248,16 @@
             else:
                 src_up = ref.at[comps, pl.ds(XP + CX - lu, lu), rows]
                 src_dn = ref.at[comps, pl.ds(XP, ld), rows]
+            stop = relays[n].at[h, :, pl.ds(0, lu)]
             up.append(pltpu.make_async_remote_copy(
-                src_up, ref.at[comps, pl.ds(XP - lu, lu), rows],
-                xs_sem.at[h, n], xr_sem.at[h, n], device_id=s_up, device_id_type=MESH))
+                src_up, stop, xs_sem.at[h, n], fr_sem.at[h, n], device_id=via, device_id_type=MESH))
+            on.append(pltpu.make_async_remote_copy(
+                stop, ref.at[comps, pl.ds(XP - lu, lu), rows],
+                fs_sem.at[h, n], xr_sem.at[h, n], device_id=onward, device_id_type=MESH))
             dn.append(pltpu.make_async_remote_copy(
                 src_dn, ref.at[comps, pl.ds(XP + CX, ld), rows],
                 xs_sem.at[h, 2 + n], xr_sem.at[h, 2 + n], device_id=s_dn, device_id_type=MESH))
-        return up, dn
+        return up, dn, on
 
     def each(there, copies, act):
         @pl.when(there)
@@ -234,19 +266,29 @@
                 act(copy)
 
     def x_start(h):
-        up, dn = x_copies(h)
+        up, dn, _ = x_copies(h)
         each(has["s_up"], up, lambda c: c.start())
         each(has["s_dn"], dn, lambda c: c.start())
 
+    def x_forward(h):
+        up, _, on = x_copies(h)
+
+        @pl.when(forwards)
+        def _():
+            for came, goes in zip(up, on):
+                came.wait_recv()
+                goes.start()
+
     def x_wait_recv(h):
-        up, dn = x_copies(h)
-        each(has["s_dn"], up, lambda c: c.wait_recv())
+        _, dn, on = x_copies(h)
+        each(has["s_dn"], on, lambda c: c.wait_recv())
         each(has["s_up"], dn, lambda c: c.wait_recv())
 
     def x_wait_send(h):
-        up, dn = x_copies(h)
+        up, dn, on = x_copies(h)
         each(has["s_up"], up, lambda c: c.wait_send())
         each(has["s_dn"], dn, lambda c: c.wait_send())
+        each(forwards, on, lambda c: c.wait_send())
 
     x_start(0)
 
@@ -578,6 +620,7 @@
     yz_send(0, 1)
     deep_part(0, 0)
     deep_part(0, 1)
+    x_forward(0)
     loads[2].wait()
     loads[3].wait()
     yz_recv(0, 0)
@@ -595,6 +638,7 @@
         copy.wait()
     yz_recv(1, 0)
     interior(stress_pair)
+    x_forward(1)
     source_gather()
     source_plane(0)
     apply_source(plane, middle)
@@ -610,6 +654,7 @@
     yz_send(2, 1)
     yz_recv(2, 0)
     interior(velocity_pair)
+    x_forward(2)
     yz_send(3, 0)
     deep_part(2, 1)
     deep_part(3, 0)
@@ -622,6 +667,7 @@
     yz_send(3, 1)
     yz_recv(3, 0)
     interior(stress_pair)
+    x_forward(3)
     apply_source(last_plane, middle)
     deep_part(3, 1)
     yz_recv(3, 1)
@@ -674,13 +720,15 @@
                 *[(pltpu.VMEM((4, 64, cz), f32), pltpu.VMEM((4, 24, cz), f32))] * 4,
                 *[(pltpu.VMEM((4, 2, cy, cz), f32), pltpu.VMEM((4, 1, cy, cz), f32))] * 3,
                 pltpu.VMEM((2, 2 * cz, cz), jnp.bfloat16),
+                pltpu.VMEM((4, 1, 2, cy, cz), f32),
+                pltpu.VMEM((4, 2, 2, cy, cz), f32),
                 pltpu.VMEM((ns // NA, STEPS, 8, 128), f32),
                 pltpu.VMEM((NA, STEPS, 8, 128), f32),
                 pltpu.VMEM((STEPS, 8, 128), f32),
                 pltpu.VMEM((nd * nh, STEPS, 8, 128), f32),
                 pltpu.VMEM((3 * 6 * cx, cz), f32),
                 pltpu.VMEM((6 * cx, cz), f32),
-                dma((12,)), dma((4, 4)), dma((4, 4)), dma((4, 2, 2)), dma((4, 2, 2)), dma((4, 2, 2)), dma((4, 2, 2)),
+                dma((4, 2)), dma((4, 2)), dma((12,)), dma((4, 4)), dma((4, 4)), dma((4, 2, 2)), dma((4, 2, 2)), dma((4, 2, 2)), dma((4, 2, 2)),
                 dma((ns // NA,)), dma((ns // NA,)), dma, dma, dma((nh,)), dma((nd * nh,)),
             ],
             compiler_params=pltpu.CompilerParams(

time: 39.9 us -> 46 us (1.15)
  the two profiles are of different devices: /device:TPU:12 before, /device:TPU:84 now
where the time goes in v3:
time: 46 us; the launch traced here: 45.9 us
  Pallas kernels  45.3 us (98%)
  between operations  0.64 us (1%)
    pallas_call x1, Pallas kernels, body(): pl.pallas_call(functools.partial(kernel, (ns, nd, nh, cx, cy, subf)), out...  43.3 us
    pallas_call x1, Pallas kernels, body(): pl.pallas_call(functools.partial(finish, (cx, cy)), out_shape=tuple((jax....  1.97 us

profile of v3, /device:TPU:84, one launch (start us, length us, event | category | flops | bytes accessed | tf_op | source)
XLA Modules:
  0.0 45.9 jit_solution(16156326326970822535)
XLA Ops:
  0.6 43.3 %shard_map.139 = (f32[6,20,48,128]{3,2,1,0:T(8,128)S(1)}, f32[3,20,48,128]{3,2,1,0:T(8,128)S(1)}, f32[6,16,32,128]{3,2,1,0:T(8,128)S(1)}, f32[3,16,32,128]{3,2,1...) custom-call(f32[3,16,32,128]{3,2,1,0:T(8,128)} %vel_hbm.1, ...), custom_call_target="tpu_custom_call" | custom-call | flops 30000000 | bytes 6000000 | tf_op jit(solution)/shard_map/pallas_call | solution.py:709
  43.9 2.0 %shard_map.140 = (f32[3,16,32,128]{3,2,1,0:T(8,128)}, f32[6,16,32,128]{3,2,1,0:T(8,128)}, f32[6,16,32,128]{3,2,1,0:T(8,128)}) custom-call(f32[6,20,48,128]{3,2,1,0:T(8,128)S(1)} %get-tuple-element.12.S, f32[3,20,48,128]{3,2,1,0:T(8,128)S(1)} %get-tuple-element.13.V, f32[6,16,32,128]{3,2,1,0:T(8,128)S(1)} %get-tuple-element.14.M, ...), custom_call_target="tpu_custom_call" | custom-call | flops 2000000 | bytes 4000000 | tf_op jit(solution)/shard_map/pallas_call | solution.py:742

commit v4 on v2

--- a/solution.py
+++ b/solution.py
@@ -108,7 +108,7 @@
     S, V, M, deep, lam, mu, rel, ane, last_plane,
     buo, rate, cells, active, offset,
     ysend_up, ysend_dn, yrecv_up, yrecv_dn, zsend, zrecv_up, zrecv_dn, band,
-    cand, pair, chosen, gathered, acc, plane,
+    cand, pair, chosen, gathered, plane,
     ld_sem, xs_sem, xr_sem, ys_sem, yr_sem, zs_sem, zr_sem,
     c_send, c_recv, p_send, p_recv, g_send, g_recv,
 ):
@@ -135,6 +135,53 @@
         "d_up": d < NH - 1, "d_dn": d > 0,
     }
 
+    barrier = pltpu.get_barrier_semaphore()
+    count = jnp.int32(0)
+    for name, to in (("s_up", s_up), ("s_dn", s_dn), ("k_up", k_up), ("k_dn", k_dn), ("d_up", d_up), ("d_dn", d_dn)):
+        there = has[name]
+        count = count + there.astype(jnp.int32)
+
+        @pl.when(there)
+        def _(to=to):
+            pl.semaphore_signal(barrier, inc=1, device_id=to, device_id_type=MESH)
+
+    other = {"strike": group * NA + lax.rem(parity + 1, NA)}
+    pl.semaphore_signal(barrier, inc=1, device_id=other, device_id_type=MESH)
+    count = count + 1
+
+    @pl.loop(0, NB)
+    def _(g):
+        @pl.when(g != group)
+        def _():
+            pl.semaphore_signal(
+                barrier, inc=1, device_id={"strike": g * NA + parity}, device_id_type=MESH
+            )
+
+    count = count + (NB - 1)
+
+    @pl.loop(0, NH)
+    def _(h):
+        @pl.when(jnp.logical_not(on_fault & (h == d)))
+        def _():
+            pl.semaphore_signal(
+                barrier, inc=1, device_id={"dip": fault, "depth": h}, device_id_type=MESH
+            )
+
+    count = count + NH - on_fault.astype(jnp.int32)
+
+    @pl.when(on_fault)
+    def _():
+        @pl.loop(0, ND * NH)
+        def _(j):
+            @pl.when(j != chunk)
+            def _():
+                pl.semaphore_signal(
+                    barrier, inc=1,
+                    device_id={"dip": lax.div(j, NH), "depth": lax.rem(j, NH)},
+                    device_id_type=MESH,
+                )
+
+    count = count + jnp.where(on_fault, ND * NH - 1, 0)
     inner = (slice(None), pl.ds(XP, CX), pl.ds(YP, CY))
     loads = [
         pltpu.make_async_copy(str_hbm, S.at[inner], ld_sem.at[0]),
@@ -157,53 +204,6 @@
     for copy in (loads[1], *order, loads[0], loads[2], loads[3]):
         copy.start()
 
-    barrier = pltpu.get_barrier_semaphore()
-    count = jnp.int32(0)
-    for name, to in (("s_up", s_up), ("s_dn", s_dn), ("k_up", k_up), ("k_dn", k_dn), ("d_up", d_up), ("d_dn", d_dn)):
-        there = has[name]
-        count = count + there.astype(jnp.int32)
-
-        @pl.when(there)
-        def _(to=to):
-            pl.semaphore_signal(barrier, inc=1, device_id=to, device_id_type=MESH)
-
-    other = {"strike": group * NA + lax.rem(parity + 1, NA)}
-    pl.semaphore_signal(barrier, inc=1, device_id=other, device_id_type=MESH)
-    count = count + 1
-
-    @pl.loop(0, NB)
-    def _(g):
-        @pl.when(g != group)
-        def _():
-            pl.semaphore_signal(
-                barrier, inc=1, device_id={"strike": g * NA + parity}, device_id_type=MESH
-            )
-
-    count = count + (NB - 1)
-
-    @pl.loop(0, NH)
-    def _(h):
-        @pl.when(jnp.logical_not(on_fault & (h == d)))
-        def _():
-            pl.semaphore_signal(
-                barrier, inc=1, device_id={"dip": fault, "depth": h}, device_id_type=MESH
-            )
-
-    count = count + NH - on_fault.astype(jnp.int32)
-
-    @pl.when(on_fault)
-    def _():
-        @pl.loop(0, ND * NH)
-        def _(j):
-            @pl.when(j != chunk)
-            def _():
-                pl.semaphore_signal(
-                    barrier, inc=1,
-                    device_id={"dip": lax.div(j, NH), "depth": lax.rem(j, NH)},
-                    device_id_type=MESH,
-                )
-
-    count = count + jnp.where(on_fault, ND * NH - 1, 0)
     pl.semaphore_wait(barrier, count)
 
     def x_copies(h):
@@ -233,22 +233,21 @@
             for copy in copies:
                 act(copy)
 
-    def x_start(h):
-        up, dn = x_copies(h)
-        each(has["s_up"], up, lambda c: c.start())
-        each(has["s_dn"], dn, lambda c: c.start())
-
-    def x_wait_recv(h):
-        up, dn = x_copies(h)
-        each(has["s_dn"], up, lambda c: c.wait_recv())
-        each(has["s_up"], dn, lambda c: c.wait_recv())
+    def x_start(h, side):
+        there = has["s_up"] if side == 0 else has["s_dn"]
+        each(there, x_copies(h)[side], lambda c: c.start())
+
+    def x_wait_recv(h, side):
+        there = has["s_dn"] if side == 0 else has["s_up"]
+        each(there, x_copies(h)[side], lambda c: c.wait_recv())
 
     def x_wait_send(h):
         up, dn = x_copies(h)
         each(has["s_up"], up, lambda c: c.wait_send())
         each(has["s_dn"], dn, lambda c: c.wait_send())
 
-    x_start(0)
+    x_start(0, 0)
+    x_start(0, 1)
 
     Sf = S.reshape(6, (CX + 2 * XP) * ROW, 128)
     Vf = V.reshape(3, (CX + 2 * XP) * ROW, 128)
@@ -438,10 +437,15 @@
         def _(i):
             one(2 * i + 2, range(0, CY, 8))
 
-    def boundary(one):
-        @pl.loop(0, 2)
-        def _(i):
-            one(i * (CX - 2), range(0, CY, 8))
+    nought = jnp.minimum(s, 0)
+
+    def edges(h, one, source=None):
+        for side, x in ((0, 0), (1, CX - 2)):
+            x_wait_recv(h, side)
+            one(nought + x, range(0, CY, 8))
+            if source is not None:
+                apply_source(source, ((x, 2),))
+            x_start(h + 1, 1 - side)
 
     def candidates():
         row = lax.broadcasted_iota(jnp.int32, (TB, 128), 0)
@@ -515,38 +519,35 @@
                 def _():
                     g_copy(j, 0).wait_recv()
 
-    def source_plane(t):
+    def source_plane(t, piece):
         @pl.when(on_fault)
         def _():
             seg = active[t]
             depth_total = 128 * NH
-            acc[...] = jnp.zeros_like(acc)
-            wide = 8 * 128
-
-            @pl.loop(0, SUBF // wide)
-            def _(i):
-                cell = cells[pl.ds(seg, 1), pl.ds(pl.multiple_of(i * wide, wide), wide)]
-                cell_x = lax.div(cell, depth_total)
-                cell_z = cell - cell_x * depth_total - d * 128
-                cell_x = cell_x - s * CX
-                hot_z = (lax.broadcasted_iota(jnp.int32, (128, wide), 0) == cell_z).astype(jnp.float32).astype(jnp.bfloat16)
-                hot_x = lax.broadcasted_iota(jnp.int32, (CX, wide), 0) == cell_x
-                value = jnp.concatenate([gathered[8 * i + n, t] for n in range(8)], axis=1)
-                parts = []
-                for _ in range(3):
-                    part = value.astype(jnp.bfloat16).astype(jnp.float32)
-                    parts.append(part)
-                    value = value - part
-                rows = [
-                    jnp.where(hot_x, part[c:c + 1, :], 0.0).astype(jnp.bfloat16)
-                    for part in parts for c in range(6)
-                ]
-                acc[...] += lax.dot_general(
-                    jnp.concatenate(rows, axis=0), hot_z, (((1,), (1,)), ((), ())),
-                    preferred_element_type=jnp.float32)
-
+            wide = SUBF // 2
+            cell = cells[pl.ds(seg, 1), piece * wide:(piece + 1) * wide]
+            cell_x = lax.div(cell, depth_total)
+            cell_z = cell - cell_x * depth_total - d * 128
+            cell_x = cell_x - s * CX
+            hot_z = (lax.broadcasted_iota(jnp.int32, (128, wide), 0) == cell_z).astype(jnp.float32).astype(jnp.bfloat16)
+            hot_x = lax.broadcasted_iota(jnp.int32, (CX, wide), 0) == cell_x
+            first = piece * wide // 128
+            value = jnp.concatenate([gathered[first + n, t] for n in range(wide // 128)], axis=1)
+            high = value.astype(jnp.bfloat16).astype(jnp.float32)
+            rows = [
+                jnp.where(hot_x, part[c:c + 1, :], 0.0).astype(jnp.bfloat16)
+                for part in (high, value - high) for c in range(6)
+            ]
+            out = lax.dot_general(
+                jnp.concatenate(rows, axis=0), hot_z, (((1,), (1,)), ((), ())),
+                preferred_element_type=jnp.float32)
             n = 6 * CX
-            (plane if t == 0 else last_plane)[...] = acc[0:n] + acc[n:2 * n] + acc[2 * n:3 * n]
+            out = out[0:n] + out[n:2 * n]
+            ref = plane if t == 0 else last_plane
+            if piece == 0:
+                ref[...] = out
+            else:
+                ref[...] = ref[...] + out
 
     def apply_source(ref, spans):
         @pl.when(on_fault)
@@ -556,7 +557,6 @@
                     at = pl.ds((x0 + XP) * ROW + YP, n, stride=ROW)
                     Sf[c, at, :] = Sf[c, at, :] - ref[c * CX + x0:c * CX + x0 + n, :]
 
-    edges = ((0, 2), (CX - 2, 2))
     middle = ((2, CX - 4),)
 
     i, j = (lax.broadcasted_iota(jnp.int32, (256, 128), n) for n in range(2))
@@ -587,48 +587,40 @@
     source_third()
     deep_part(1, 0)
     yz_recv(0, 1)
-    x_wait_recv(0)
-    boundary(velocity_pair)
-    x_start(1)
+    edges(0, velocity_pair)
     yz_send(1, 1)
     for copy in loads[4:]:
         copy.wait()
     yz_recv(1, 0)
     interior(stress_pair)
     source_gather()
-    source_plane(0)
+    source_plane(0, 0)
+    source_plane(0, 1)
     apply_source(plane, middle)
     yz_send(2, 0)
     deep_part(1, 1)
     deep_part(2, 0)
     x_wait_send(0)
     yz_recv(1, 1)
-    x_wait_recv(1)
-    boundary(stress_pair)
-    apply_source(plane, edges)
-    x_start(2)
+    edges(1, stress_pair, plane)
     yz_send(2, 1)
     yz_recv(2, 0)
     interior(velocity_pair)
     yz_send(3, 0)
     deep_part(2, 1)
     deep_part(3, 0)
-    source_plane(1)
+    source_plane(1, 0)
     x_wait_send(1)
     yz_recv(2, 1)
-    x_wait_recv(2)
-    boundary(velocity_pair)
-    x_start(3)
+    edges(2, velocity_pair)
     yz_send(3, 1)
     yz_recv(3, 0)
     interior(stress_pair)
+    source_plane(1, 1)
     apply_source(last_plane, middle)
     deep_part(3, 1)
     yz_recv(3, 1)
-    x_wait_recv(3)
-
     x_wait_send(2)
-    x_wait_send(3)
     for h in range(4):
         for part in range(2):
             for there, pair_of in (("k", y_copies(h, part)), ("d", z_copies(h, part))):
@@ -637,6 +629,9 @@
     over_groups(lambda g: c_copy(group, g).wait_send())
     pair_copy(parity).wait_send()
     over_fault(lambda h: g_copy(chunk, h).wait_send())
+    x_wait_recv(3, 0)
+    x_wait_recv(3, 1)
+    x_wait_send(3)
 
 
 def solution(mesh):
@@ -678,7 +673,6 @@
                 pltpu.VMEM((NA, STEPS, 8, 128), f32),
                 pltpu.VMEM((STEPS, 8, 128), f32),
                 pltpu.VMEM((nd * nh, STEPS, 8, 128), f32),
-                pltpu.VMEM((3 * 6 * cx, cz), f32),
                 pltpu.VMEM((6 * cx, cz), f32),
                 dma((12,)), dma((4, 4)), dma((4, 4)), dma((4, 2, 2)), dma((4, 2, 2)), dma((4, 2, 2)), dma((4, 2, 2)),
                 dma((ns // NA,)), dma((ns // NA,)), dma, dma, dma((nh,)), dma((nd * nh,)),

time: 39.9 us -> 39.4 us (0.987)
  Pallas kernels: 39.2 us -> 38.5 us
    pallas_call x1, Pallas kernels: 37.2 us -> 36.5 us  [body(): pl.pallas_call(functools.partial(kernel, (ns, nd, nh, cx, cy, subf)), out...]
where the time goes in v4:
time: 39.4 us; the launch traced here: 39.1 us
  Pallas kernels  38.5 us (98%)
  between operations  0.64 us (2%)
    pallas_call x1, Pallas kernels, body(): pl.pallas_call(functools.partial(kernel, (ns, nd, nh, cx, cy, subf)), out...  36.5 us
    pallas_call x1, Pallas kernels, body(): pl.pallas_call(functools.partial(finish, (cx, cy)), out_shape=tuple((jax....  1.97 us

profile of v4, /device:TPU:12, one launch (start us, length us, event | category | flops | bytes accessed | tf_op | source)
XLA Modules:
  0.0 39.1 jit_solution(10742758741784539678)
XLA Ops:
  0.6 36.5 %shard_map.139 = (f32[6,20,48,128]{3,2,1,0:T(8,128)S(1)}, f32[3,20,48,128]{3,2,1,0:T(8,128)S(1)}, f32[6,16,32,128]{3,2,1,0:T(8,128)S(1)}, f32[3,16,32,128]{3,2,1...) custom-call(f32[3,16,32,128]{3,2,1,0:T(8,128)} %vel_hbm.1, ...), custom_call_target="tpu_custom_call" | custom-call | flops 30000000 | bytes 6000000 | tf_op jit(solution)/shard_map/pallas_call | solution.py:658
  37.2 2.0 %shard_map.140 = (f32[3,16,32,128]{3,2,1,0:T(8,128)}, f32[6,16,32,128]{3,2,1,0:T(8,128)}, f32[6,16,32,128]{3,2,1,0:T(8,128)}) custom-call(f32[6,20,48,128]{3,2,1,0:T(8,128)S(1)} %get-tuple-element.12.S, f32[3,20,48,128]{3,2,1,0:T(8,128)S(1)} %get-tuple-element.13.V, f32[6,16,32,128]{3,2,1,0:T(8,128)S(1)} %get-tuple-element.14.M, ...), custom_call_target="tpu_custom_call" | custom-call | flops 2000000 | bytes 4000000 | tf_op jit(solution)/shard_map/pallas_call | solution.py:688

commit v5 on v4

--- a/solution.py
+++ b/solution.py
@@ -247,7 +247,6 @@
         each(has["s_dn"], dn, lambda c: c.wait_send())
 
     x_start(0, 0)
-    x_start(0, 1)
 
     Sf = S.reshape(6, (CX + 2 * XP) * ROW, 128)
     Vf = V.reshape(3, (CX + 2 * XP) * ROW, 128)
@@ -440,7 +439,8 @@
     nought = jnp.minimum(s, 0)
 
     def edges(h, one, source=None):
-        for side, x in ((0, 0), (1, CX - 2)):
+        sides = ((0, 0), (1, CX - 2))
+        for side, x in sides if h % 2 == 0 else sides[::-1]:
             x_wait_recv(h, side)
             one(nought + x, range(0, CY, 8))
             if source is not None:
@@ -576,6 +576,7 @@
         copy.start()
     yz_send(0, 0)
     yz_send(0, 1)
+    x_start(0, 1)
     deep_part(0, 0)
     deep_part(0, 1)
     loads[2].wait()

time: 39.4 us -> 39.4 us (level)
  no operation moved by 1% of the time
where the time goes in v5:
time: 39.4 us; the launch traced here: 39.3 us
  Pallas kernels  38.7 us (98%)
  between operations  0.64 us (2%)
    pallas_call x1, Pallas kernels, body(): pl.pallas_call(functools.partial(kernel, (ns, nd, nh, cx, cy, subf)), out...  36.7 us
    pallas_call x1, Pallas kernels, body(): pl.pallas_call(functools.partial(finish, (cx, cy)), out_shape=tuple((jax....  1.97 us

profile of v5, /device:TPU:12, one launch (start us, length us, event | category | flops | bytes accessed | tf_op | source)
XLA Modules:
  0.0 39.3 jit_solution(2745228560422054314)
XLA Ops:
  0.6 36.7 %shard_map.139 = (f32[6,20,48,128]{3,2,1,0:T(8,128)S(1)}, f32[3,20,48,128]{3,2,1,0:T(8,128)S(1)}, f32[6,16,32,128]{3,2,1,0:T(8,128)S(1)}, f32[3,16,32,128]{3,2,1...) custom-call(f32[3,16,32,128]{3,2,1,0:T(8,128)} %vel_hbm.1, ...), custom_call_target="tpu_custom_call" | custom-call | flops 30000000 | bytes 6000000 | tf_op jit(solution)/shard_map/pallas_call | solution.py:659
  37.4 2.0 %shard_map.140 = (f32[3,16,32,128]{3,2,1,0:T(8,128)}, f32[6,16,32,128]{3,2,1,0:T(8,128)}, f32[6,16,32,128]{3,2,1,0:T(8,128)}) custom-call(f32[6,20,48,128]{3,2,1,0:T(8,128)S(1)} %get-tuple-element.12.S, f32[3,20,48,128]{3,2,1,0:T(8,128)S(1)} %get-tuple-element.13.V, f32[6,16,32,128]{3,2,1,0:T(8,128)S(1)} %get-tuple-element.14.M, ...), custom_call_target="tpu_custom_call" | custom-call | flops 2000000 | bytes 4000000 | tf_op jit(solution)/shard_map/pallas_call | solution.py:689

commit v6 on v5

--- a/solution.py
+++ b/solution.py
@@ -15,7 +15,7 @@
 YP = 8
 NA = 2
 
-X_GROUPS = {"s": ((0, 1, 1, 2), (3, 2, 2, 1)), "v": ((0, 1, 2, 1), (1, 2, 1, 2))}
+X_GROUPS = {"s": ((0, 1, 1, 2), (3, 2, 2, 1)), "v": ((0, 3, 2, 2),)}
 Y_FIELDS = {"s": ((3, True), (5, True), (1, False)), "v": ((1, True), (0, False), (2, False))}
 Z_FIELDS = {"s": (4, 5, 2), "v": (0, 1, 2)}
 Z_BACK = {"s": (True, True, False), "v": (False, False, True)}
@@ -146,8 +146,6 @@
             pl.semaphore_signal(barrier, inc=1, device_id=to, device_id_type=MESH)
 
     other = {"strike": group * NA + lax.rem(parity + 1, NA)}
-    pl.semaphore_signal(barrier, inc=1, device_id=other, device_id_type=MESH)
-    count = count + 1
 
     @pl.loop(0, NB)
     def _(g):
@@ -158,14 +156,6 @@
             )
 
     count = count + (NB - 1)
-
-    @pl.loop(0, NH)
-    def _(h):
-        @pl.when(jnp.logical_not(on_fault & (h == d)))
-        def _():
-            pl.semaphore_signal(
-                barrier, inc=1, device_id={"dip": fault, "depth": h}, device_id_type=MESH
-            )
 
     count = count + NH - on_fault.astype(jnp.int32)
 
@@ -181,7 +171,6 @@
                     device_id_type=MESH,
                 )
 
-    count = count + jnp.where(on_fault, ND * NH - 1, 0)
     inner = (slice(None), pl.ds(XP, CX), pl.ds(YP, CY))
     loads = [
         pltpu.make_async_copy(str_hbm, S.at[inner], ld_sem.at[0]),

time: 39.4 us -> 40.5 us (1.028); the launches traced: 39.3 us -> 40 us
  Pallas kernels: 38.7 us -> 39.3 us
    pallas_call x1, Pallas kernels: 36.7 us -> 37.3 us  [body(): pl.pallas_call(functools.partial(kernel, (ns, nd, nh, cx, cy, subf)), out...]
where the time goes in v6:
time: 40.5 us; the launch traced here: 40 us
  Pallas kernels  39.3 us (97%)
  between operations  0.64 us (2%)
    pallas_call x1, Pallas kernels, body(): pl.pallas_call(functools.partial(kernel, (ns, nd, nh, cx, cy, subf)), out...  37.3 us
    pallas_call x1, Pallas kernels, body(): pl.pallas_call(functools.partial(finish, (cx, cy)), out_shape=tuple((jax....  1.97 us

profile of v6, /device:TPU:12, one launch (start us, length us, event | category | flops | bytes accessed | tf_op | source)
XLA Modules:
  0.0 40.0 jit_solution(1824860053996588453)
XLA Ops:
  0.6 37.3 %shard_map.139 = (f32[6,20,48,128]{3,2,1,0:T(8,128)S(1)}, f32[3,20,48,128]{3,2,1,0:T(8,128)S(1)}, f32[6,16,32,128]{3,2,1,0:T(8,128)S(1)}, f32[3,16,32,128]{3,2,1...) custom-call(f32[3,16,32,128]{3,2,1,0:T(8,128)} %vel_hbm.1, ...), custom_call_target="tpu_custom_call" | custom-call | flops 30000000 | bytes 6000000 | tf_op jit(solution)/shard_map/pallas_call | solution.py:648
  38.0 2.0 %shard_map.140 = (f32[3,16,32,128]{3,2,1,0:T(8,128)}, f32[6,16,32,128]{3,2,1,0:T(8,128)}, f32[6,16,32,128]{3,2,1,0:T(8,128)}) custom-call(f32[6,20,48,128]{3,2,1,0:T(8,128)S(1)} %get-tuple-element.12.S, f32[3,20,48,128]{3,2,1,0:T(8,128)S(1)} %get-tuple-element.13.V, f32[6,16,32,128]{3,2,1,0:T(8,128)S(1)} %get-tuple-element.14.M, ...), custom_call_target="tpu_custom_call" | custom-call | flops 2000000 | bytes 4000000 | tf_op jit(solution)/shard_map/pallas_call | solution.py:678

commit v7 on v6

--- a/solution.py
+++ b/solution.py
@@ -15,7 +15,7 @@
 YP = 8
 NA = 2
 
-X_GROUPS = {"s": ((0, 1, 1, 2), (3, 2, 2, 1)), "v": ((0, 3, 2, 2),)}
+X_GROUPS = {"s": ((0, 1, 1, 2), (3, 2, 2, 1)), "v": ((0, 1, 2, 1), (1, 2, 1, 2))}
 Y_FIELDS = {"s": ((3, True), (5, True), (1, False)), "v": ((1, True), (0, False), (2, False))}
 Z_FIELDS = {"s": (4, 5, 2), "v": (0, 1, 2)}
 Z_BACK = {"s": (True, True, False), "v": (False, False, True)}

time: 40.5 us -> 39.3 us (0.970); the launches traced: 40 us -> 39.2 us
  Pallas kernels: 39.3 us -> 38.6 us
    pallas_call x1, Pallas kernels: 37.3 us -> 36.6 us  [body(): pl.pallas_call(functools.partial(kernel, (ns, nd, nh, cx, cy, subf)), out...]
where the time goes in v7:
time: 39.3 us; the launch traced here: 39.2 us
  Pallas kernels  38.6 us (98%)
  between operations  0.64 us (2%)
    pallas_call x1, Pallas kernels, body(): pl.pallas_call(functools.partial(kernel, (ns, nd, nh, cx, cy, subf)), out...  36.6 us
    pallas_call x1, Pallas kernels, body(): pl.pallas_call(functools.partial(finish, (cx, cy)), out_shape=tuple((jax....  1.97 us

profile of v7, /device:TPU:12, one launch (start us, length us, event | category | flops | bytes accessed | tf_op | source)
XLA Modules:
  0.0 39.2 jit_solution(5198006381418195456)
XLA Ops:
  0.6 36.6 %shard_map.139 = (f32[6,20,48,128]{3,2,1,0:T(8,128)S(1)}, f32[3,20,48,128]{3,2,1,0:T(8,128)S(1)}, f32[6,16,32,128]{3,2,1,0:T(8,128)S(1)}, f32[3,16,32,128]{3,2,1...) custom-call(f32[3,16,32,128]{3,2,1,0:T(8,128)} %vel_hbm.1, ...), custom_call_target="tpu_custom_call" | custom-call | flops 30000000 | bytes 6000000 | tf_op jit(solution)/shard_map/pallas_call | solution.py:648
  37.2 2.0 %shard_map.140 = (f32[3,16,32,128]{3,2,1,0:T(8,128)}, f32[6,16,32,128]{3,2,1,0:T(8,128)}, f32[6,16,32,128]{3,2,1,0:T(8,128)}) custom-call(f32[6,20,48,128]{3,2,1,0:T(8,128)S(1)} %get-tuple-element.12.S, f32[3,20,48,128]{3,2,1,0:T(8,128)S(1)} %get-tuple-element.13.V, f32[6,16,32,128]{3,2,1,0:T(8,128)S(1)} %get-tuple-element.14.M, ...), custom_call_target="tpu_custom_call" | custom-call | flops 2000000 | bytes 4000000 | tf_op jit(solution)/shard_map/pallas_call | solution.py:678

commit v8 on v7

--- a/solution.py
+++ b/solution.py
@@ -327,11 +327,24 @@
                 where, index = z_slot(part, place, n)
                 value = F[comp, pl.ds((x + XP) * ROW + YP, CY), :]
                 arrays[where] = jnp.where(slot == index, turn(value, 4 * index + 2), arrays[where])
-        for n, value in enumerate(arrays):
-            zsend[part][h, n] = value
+        half = CY // 2
+        last = arrays[-1]
+        folded = jnp.where(lane[:half] < 64, last[:half], turn(last[half:], 64))
+        if part == 0:
+            zsend[0][h, 0:CY, :] = arrays[0]
+            zsend[0][h, CY:CY + half, :] = folded
+        else:
+            zsend[1][h] = folded
         up, dn = z_copies(h, part)
         each(has["d_up"], [up], lambda c: c.start())
         each(has["d_dn"], [dn], lambda c: c.start())
+
+    def z_got(refs, h, part, where):
+        if part == 0 and where == 0:
+            return refs[0][h, 0:CY, :]
+        at = CY if part == 0 else 0
+        value = refs[part][h, at:at + CY // 2, :]
+        return jnp.concatenate([value, turn(value, -64)], axis=0)
 
     def yz_recv(h, part):
         kind = "sv"[h % 2]
@@ -355,7 +368,7 @@
             for n, x in enumerate(PLANES[part]):
                 where, index = z_slot(part, place, n)
                 if (where, back) not in fixes:
-                    mix = jnp.where(quarter < 2, zrecv_up[part][h, where], zrecv_dn[part][h, where])
+                    mix = jnp.where(quarter < 2, z_got(zrecv_up, h, part, where), z_got(zrecv_dn, h, part, where))
                     below, two_after = turn(mix, 1), turn(mix, -2)
                     if back:
                         fix = jnp.where(quarter == 0, -two_after, jnp.where(quarter == 1, below - 27.0 * mix, below))
@@ -657,7 +670,7 @@
                 pltpu.SMEM(active.shape, jnp.int32),
                 pltpu.SMEM(offset.shape, jnp.int32),
                 *[(pltpu.VMEM((4, 64, cz), f32), pltpu.VMEM((4, 24, cz), f32))] * 4,
-                *[(pltpu.VMEM((4, 2, cy, cz), f32), pltpu.VMEM((4, 1, cy, cz), f32))] * 3,
+                *[(pltpu.VMEM((4, cy + cy // 2, cz), f32), pltpu.VMEM((4, cy // 2, cz), f32))] * 3,
                 pltpu.VMEM((2, 2 * cz, cz), jnp.bfloat16),
                 pltpu.VMEM((ns // NA, STEPS, 8, 128), f32),
                 pltpu.VMEM((NA, STEPS, 8, 128), f32),

time: 39.3 us -> 39.2 us (level)
  no operation moved by 1% of the time
where the time goes in v8:
time: 39.2 us; the launch traced here: 39.1 us
  Pallas kernels  38.4 us (98%)
  between operations  0.64 us (2%)
    pallas_call x1, Pallas kernels, body(): pl.pallas_call(functools.partial(kernel, (ns, nd, nh, cx, cy, subf)), out...  36.4 us
    pallas_call x1, Pallas kernels, body(): pl.pallas_call(functools.partial(finish, (cx, cy)), out_shape=tuple((jax....  1.97 us

profile of v8, /device:TPU:12, one launch (start us, length us, event | category | flops | bytes accessed | tf_op | source)
XLA Modules:
  0.0 39.1 jit_solution(7510193792145750484)
XLA Ops:
  0.6 36.4 %shard_map.139 = (f32[6,20,48,128]{3,2,1,0:T(8,128)S(1)}, f32[3,20,48,128]{3,2,1,0:T(8,128)S(1)}, f32[6,16,32,128]{3,2,1,0:T(8,128)S(1)}, f32[3,16,32,128]{3,2,1...) custom-call(f32[3,16,32,128]{3,2,1,0:T(8,128)} %vel_hbm.1, ...), custom_call_target="tpu_custom_call" | custom-call | flops 30000000 | bytes 6000000 | tf_op jit(solution)/shard_map/pallas_call | solution.py:661
  37.1 2.0 %shard_map.140 = (f32[3,16,32,128]{3,2,1,0:T(8,128)}, f32[6,16,32,128]{3,2,1,0:T(8,128)}, f32[6,16,32,128]{3,2,1,0:T(8,128)}) custom-call(f32[6,20,48,128]{3,2,1,0:T(8,128)S(1)} %get-tuple-element.12.S, f32[3,20,48,128]{3,2,1,0:T(8,128)S(1)} %get-tuple-element.13.V, f32[6,16,32,128]{3,2,1,0:T(8,128)S(1)} %get-tuple-element.14.M, ...), custom_call_target="tpu_custom_call" | custom-call | flops 2000000 | bytes 4000000 | tf_op jit(solution)/shard_map/pallas_call | solution.py:691
